TPU v7x, 256 devices: a whole 4x4x8 slice. The times are simulated.
256 devices in a mesh: wide: 32 (over z, y), narrow: 8 (over x, core).
Axes of the slice: x: 4, y: 4, z: 8, core: 2. Of those that a mesh axis runs over, the one named last changes fastest.
Arguments:
- spins: int32 [4096, 4096], P('wide'), may hold values from -1 to 1, as said below
- weights: bfloat16 [4096, 8192], P('wide', 'narrow'), may hold values from -0.09375 to 0.09375
- field_bias: float32 [8192], P('narrow'), may hold values from -3 to 3
- energies: bfloat16 [4096], P('wide')
- panel_index: int32 [1], replicated, may hold values from 0 to 3
- diag_inverse: bfloat16 [1024, 1024], replicated, as said below
Outputs:
- grad_w: float32 [4096, 8192], P('wide', 'narrow')
- panel_factor: bfloat16 [4096, 1024], P(('wide', 'narrow'))
- update: float32 [4096], P(('wide', 'narrow'))
Inputs may be any that keep to these rules, and one draw needn't show every extreme that they name: `spins`: each entry is +1 or -1. `diag_inverse`: lower triangular.
All inputs are finite; a program needn't handle non-finite values.
Results may differ from a plain program's by a relative error of at most 0.025.
Values may be sent and summed in bfloat16 or wider, within the bound.
A program may use at most 64 MiB of HBM per device.

v0:
```python
import math

import jax
import jax.numpy as jnp
from jax import lax
from jax.sharding import PartitionSpec as P

SPIN_SITES = 4096
HIDDEN_UNITS = 8192
PANEL_ROWS = 1024


def from_root(x, axis, root):
    mine = lax.axis_index(axis) == root
    return lax.psum(jnp.where(mine, x, jnp.zeros_like(x)), axis)


def local(spins, weights, field_bias, energies, panel_index, diag_inverse):
    wide_count = lax.axis_size("wide")
    narrow_count = lax.axis_size("narrow")
    local_rows = spins.shape[0]
    slice_width = SPIN_SITES // narrow_count
    owners = PANEL_ROWS // local_rows
    total_samples = local_rows * wide_count
    share_rows = local_rows // narrow_count
    spin_values = spins.astype(jnp.bfloat16)
    wide_pos = lax.axis_index("wide")
    narrow_pos = lax.axis_index("narrow")
    columns = spin_values
    field_sum = jnp.dot(
        columns,
        lax.all_gather(weights, "wide", axis=0, tiled=True),
        preferred_element_type=jnp.float32,
    )
    fields = jnp.tanh(field_sum + field_bias[None, :]).astype(jnp.bfloat16)
    energy_mean = lax.psum(jnp.sum(energies.astype(jnp.float32)), "wide") / total_samples
    spin_slice = lax.dynamic_slice_in_dim(spin_values, narrow_pos * slice_width, slice_width, 1)
    panel_block = panel_index[0]
    spin_parts = []
    field_parts = []
    energy_parts = []
    for offset in range(owners):
        received = (
            from_root(spin_slice, "wide", panel_block * owners + offset),
            from_root(fields, "wide", panel_block * owners + offset),
            from_root(energies, "wide", panel_block * owners + offset),
        )
        spin_parts.append(received[0])
        field_parts.append(received[1])
        energy_parts.append(received[2])
    panel_spins = jnp.concatenate(spin_parts, 0)
    panel_fields = jnp.concatenate(field_parts, 0)
    panel_energy = jnp.concatenate(energy_parts, 0)
    energy_panel = panel_energy.astype(jnp.float32) - energy_mean
    solved_panel = jnp.dot(
        diag_inverse.astype(jnp.float32), energy_panel, precision=lax.Precision.HIGHEST
    )
    contract = (((1,), (1,)), ((), ()))
    spin_gram = lax.dot_general(
        spin_slice, panel_spins, contract, preferred_element_type=jnp.float32
    )
    field_gram = lax.dot_general(fields, panel_fields, contract, preferred_element_type=jnp.float32)
    first_panel_row = panel_block * PANEL_ROWS
    spin_total, field_total = (
        lax.psum(spin_gram.astype(jnp.bfloat16), "narrow").astype(jnp.float32),
        lax.psum(field_gram.astype(jnp.bfloat16), "narrow").astype(jnp.float32),
    )
    gram_column = (spin_total / SPIN_SITES * (field_total / HIDDEN_UNITS)).astype(jnp.bfloat16)
    factor_exact = lax.dot_general(
        gram_column, diag_inverse, contract, preferred_element_type=jnp.float32
    )
    global_rows = wide_pos * local_rows + lax.iota(jnp.int32, factor_exact.shape[0])
    relative = global_rows - first_panel_row
    in_panel = (relative >= 0) & (relative < PANEL_ROWS)
    picked = solved_panel[jnp.clip(relative, 0, PANEL_ROWS - 1)]
    carried = jnp.dot(factor_exact, solved_panel, precision=lax.Precision.HIGHEST)
    coefficient = jnp.where(in_panel, picked, energies.astype(jnp.float32) - energy_mean - carried)
    factor_exact, update_all = (factor_exact, coefficient)
    factor_out = lax.dynamic_slice_in_dim(
        factor_exact, narrow_pos * share_rows, share_rows, 0
    ).astype(jnp.bfloat16)
    update_out = lax.dynamic_slice_in_dim(update_all, narrow_pos * share_rows, share_rows, 0)
    weighted = (fields.astype(jnp.float32) * update_all[:, None]).astype(jnp.bfloat16)
    columns = spin_values
    grad_rows = lax.psum_scatter(
        lax.dot_general(
            columns, weighted, (((0,), (0,)), ((), ())), preferred_element_type=jnp.float32
        ).astype(jnp.bfloat16),
        "wide",
        scatter_dimension=0,
        tiled=True,
    ).astype(jnp.float32)
    grad_w = grad_rows / math.sqrt(total_samples)
    return (grad_w, factor_out, update_out)


def solution(mesh):
    in_specs = (P("wide", None), P("wide", "narrow"), P("narrow"), P("wide"), P(), P())
    out_specs = (P("wide", "narrow"), P(("wide", "narrow"), None), P(("wide", "narrow")))
    return jax.shard_map(local, mesh=mesh, in_specs=in_specs, out_specs=out_specs, check_vma=False)
```

profile of v0, /device:TPU:2, one launch (start us, length us, event | category | flops | bytes accessed | tf_op | source)
XLA Modules:
  0.0 610.4 jit_solution(1350391532889324241)
XLA Ops:
  7.2 0.0 copy-start
  7.2 0.0 all-gather.2.cloned.1.call-start
  7.2 0.7 all-gather.2.cloned.1.call-update
  7.9 0.0 all-reduce.6.cloned.1.call-start
  8.6 0.0 copy-start.10
  8.6 1.7 convert_element_type.47
  10.4 1.0 broadcast_select_fusion.8
  11.4 100.7 %all-gather.2.cloned.1.call-done = bf16[4096,1024]{1,0:T(8,128)(2,1)} async-done(((bf16[128,1024]{1,0:T(8,128)(2,1)}), bf16[4096,1024]{1,0:T(8,128)(2,1)}) %all-gather.2.cloned.1.call-update) | async-done | bytes 8388624 | tf_op jit(solution)/shard_map/all_gather | solution.py:32
  112.1 0.0 copy-done.10
  112.1 6.1 %broadcast_select_fusion = (bf16[128,1024]{1,0:T(8,128)(2,1)}, bf16[128,1024]{1,0:T(8,128)(2,1)}, bf16[128,1024]{1,0:T(8,128)(2,1)}, bf16[128,1024]{1,0:T(8,128)...) fusion(pred[]{:T(512)S(6)} %eq.23, pred[]{:T(512)S(6)} %eq.22, ...), kind=kOutput, calls=%fused_computation.17 | convolution fusion | flops 1075052544 | bytes 11800584 | tf_op jit(solution)/shard_map/dot_general | solution.py:30
  118.3 0.0 all-reduce.6.cloned.1.call-update
  118.3 0.0 all-reduce.8.cloned.1.call-start
  118.3 0.6 copy-done.11
  118.9 0.6 convert_reduce_fusion
  119.5 72.0 %psum.197 = f32[]{:T(128)} all-reduce(f32[]{:T(128)} %convert_reduce_fusion), channel_id=1, replica_groups=mesh['wide'=32,'narrow'=8] {'wide'}, use_global_device_ids=true, to_apply=%region_9.10 | all-reduce | flops 1 | bytes 8 | tf_op jit(solution)/shard_map/psum | solution.py:36
  192.2 70.4 %all-reduce = (bf16[128]{0:T(256)(128)(2,1)S(1)}, bf16[128]{0:T(256)(128)(2,1)S(1)}, bf16[128]{0:T(256)(128)(2,1)S(1)}, bf16[128]{0:T(256)(128)(2,1)S(1)}, bf16[...) all-reduce(bf16[128]{0:T(256)(128)(2,1)S(1)} %get-tuple-element.61,, ...), channel_id=1, replica_groups=mesh['wide'=32,'narrow'=8] {'wide'}, use_global_device_ids=true, to_apply=%region_0.0 | all-reduce | flops 1024 | bytes 4096 | tf_op jit(solution)/shard_map/psum | solution.py:15
  262.7 0.2 dynamic-update-slice.16
  262.9 0.2 dynamic-update-slice.17
  263.1 0.2 dynamic-update-slice.18
  263.3 0.2 dynamic-update-slice.19
  263.4 0.2 dynamic-update-slice.20
  263.6 0.2 dynamic-update-slice.21
  263.8 0.2 dynamic-update-slice.22
  264.0 0.2 dynamic-update-slice.23
  264.2 12.7 %all-reduce.6.cloned.1.call-done = (bf16[128,1024]{1,0:T(8,128)(2,1)}, bf16[128,1024]{1,0:T(8,128)(2,1)}, bf16[128,1024]{1,0:T(8,128)(2,1)}, bf16[128,1024]{1,0:...) async-done(((bf16[128,1024]{1,0:T(8,128)(2,1)}, ...) | async-done | bytes 3145744 | tf_op jit(solution)/shard_map/psum | solution.py:15
  276.9 1.0 constant_dynamic-update-slice_fusion.7
  277.9 0.9 constant_dynamic-update-slice_fusion.6
  278.8 0.0 copy-start.7
  278.8 1.0 constant_dynamic-update-slice_fusion.5
  279.8 0.9 constant_dynamic-update-slice_fusion.4
  280.7 0.0 copy-start.6
  280.7 1.0 constant_dynamic-update-slice_fusion.3
  281.7 0.9 constant_dynamic-update-slice_fusion.2
  282.6 0.0 copy-start.5
  282.6 1.0 constant_dynamic-update-slice_fusion.1
  283.6 0.9 constant_dynamic-update-slice_fusion
  284.5 0.0 copy-start.4
  284.5 0.0 copy-start.3
  284.5 1.2 convolution_convert_fusion.1
  285.7 0.0 copy-done.9
  285.7 0.0 copy-done.8
  285.8 0.0 copy-done.7
  285.8 0.0 copy-done.6
  285.8 0.0 copy-done.5
  285.9 0.0 copy-done.4
  285.9 0.7 copy-done.2
  286.7 1.6 convolution_convert_fusion
  288.2 0.0 all-reduce.8.cloned.1.call-update
  288.2 0.0 reduce-scatter.4.cloned.1.call-start
  288.3 1.7 fusion.14
  290.0 1.0 gather_fusion
  291.0 59.2 %all-reduce.8.cloned.1.call-done = (bf16[128,1024]{1,0:T(8,128)(2,1)}, bf16[128,1024]{1,0:T(8,128)(2,1)}) async-done(((bf16[128,1024]{1,0:T(8,128)(2,1)}, bf16[128,1024]{1,0:T(8,128)(2,1)}), (bf16[128,1024]{1,0:T(8,128)(2,1)}, bf16[128,1024]{1,0:T(8,128)(2,1)})) %all-reduce.8.cloned.1.call-update) | async-done | bytes 524304 | tf_op jit(solution)/shard_map/psum | solution.py:66
  350.2 1.9 fusion.4
  352.1 0.0 copy-start.1
  352.1 0.8 copy-done.1
  352.9 0.5 fusion.3
  353.4 5.7 convert_bitcast_fusion
  359.1 12.0 %copy.12 = bf16[4096,1024]{1,0:T(8,128)(2,1)} copy(bf16[4096,1024]{0,1:T(8,128)(2,1)} %convert_bitcast_fusion) | data formatting | bytes 16777216
  371.1 0.0 reduce-scatter.4.cloned.1.call-update
  371.1 0.6 dynamic_slice.11
  371.7 1.5 dynamic-slice_convert_fusion
  373.2 228.5 %reduce-scatter.4.cloned.1.call-done = bf16[128,1024]{1,0:T(8,128)(2,1)} async-done(((bf16[4096,1024]{1,0:T(8,128)(2,1)}), bf16[128,1024]{1,0:T(8,128)(2,1)}) %reduce-scatter.4.cloned.1.call-update) | async-done | bytes 262160
  601.7 1.1 copy.13
  602.8 1.0 copy.11
  (20 shorter events, 0.2 us)
Async XLA Ops:
  7.2 281.1 %copy-start = (bf16[1024,1024]{1,0:T(8,128)(2,1)S(1)}, bf16[1024,1024]{1,0:T(8,128)(2,1)}, u32[]{:S(2)}) copy-start(bf16[1024,1024]{1,0:T(8,128)(2,1)} %param.11) | copy-start | bytes 6291460
  7.2 105.0 %all-gather.2.cloned.1.call-start = ((), (), s32[]{:S(2)}) async-start(), calls=%async_computation.1 | async-start | bytes 8650752 | tf_op jit(solution)/shard_map/all_gather | solution.py:32
  7.9 269.0 %all-reduce.6.cloned.1.call-start = ((), (), s32[]{:S(2)}) async-start(), calls=%async_computation.3 | async-start | bytes 6291456 | tf_op jit(solution)/shard_map/psum | solution.py:15
  8.6 103.5 %copy-start.10 = (f32[1024]{0:T(1024)S(1)}, f32[1024]{0:T(1024)}, u32[]{:S(2)}) copy-start(f32[1024]{0:T(1024)} %param.8) | copy-start | bytes 12292
  118.3 0.7 copy-start.11
  118.3 231.9 %all-reduce.8.cloned.1.call-start = ((), (), s32[]{:S(2)}) async-start(), calls=%async_computation.4 | async-start | bytes 1048576 | tf_op jit(solution)/shard_map/psum | solution.py:66
  276.9 8.8 %copy-start.9 = (bf16[128,1024]{1,0:T(8,128)(2,1)S(1)}, bf16[128,1024]{1,0:T(8,128)(2,1)}, u32[]{:S(2)}) copy-start(bf16[128,1024]{1,0:T(8,128)(2,1)} %get-tuple-element.20) | copy-start | bytes 786436
  276.9 8.8 %copy-start.8 = (bf16[128,1024]{1,0:T(8,128)(2,1)S(1)}, bf16[128,1024]{1,0:T(8,128)(2,1)}, u32[]{:S(2)}) copy-start(bf16[128,1024]{1,0:T(8,128)(2,1)} %get-tuple-element.21) | copy-start | bytes 786436
  278.8 6.9 %copy-start.7 = (bf16[128,1024]{1,0:T(8,128)(2,1)S(1)}, bf16[128,1024]{1,0:T(8,128)(2,1)}, u32[]{:S(2)}) copy-start(bf16[128,1024]{1,0:T(8,128)(2,1)} %get-tuple-element.22) | copy-start | bytes 786436
  280.7 5.1 copy-start.6
  282.6 3.2 copy-start.5
  284.5 1.4 copy-start.4
  284.5 1.4 copy-start.3
  285.7 0.9 copy-start.2
  288.2 313.4 %reduce-scatter.4.cloned.1.call-start = ((), (), s32[]{:S(2)}) async-start(), calls=%async_computation.2 | async-start | bytes 8650752
  352.1 0.8 copy-start.1
Sparse Core Ops, SparseCore 0:
  10.6 101.4 all-gather.1
  118.4 158.4 all-reduce.5
  288.4 61.8 all-reduce.7
  371.2 230.3 reduce-scatter.3
where the time goes:
time: 611 us; the launch traced here: 610 us
  waiting for transfers between devices  402 us (66%)
  blocking collectives  142 us (23%)
  local copies, waits for them, and re-layouts  28.4 us (5%)
  matrix products  18.7 us (3%)
  between operations  15.4 us (3%)
    unnamed x5, waiting for transfers between devices  229 us
    all_gather x1, waiting for transfers between devices, local(): lax.all_gather(weights, 'wide', axis=0, tiled=True)  101 us
    psum x1, blocking collectives, local(): lax.psum(jnp.sum(energies.astype(jnp.float32)), 'wide') / total_samples  72 us
    psum x1, blocking collectives, from_root(): return lax.psum(jnp.where(mine, x, jnp.zeros_like(x)), axis)  70.4 us
    psum x1, waiting for transfers between devices, local(): lax.psum(field_gram.astype(jnp.bfloat16), 'narrow').astype(jnp.float32)  59.2 us
    unnamed x48, local copies, waits for them, and re-layouts  24.3 us
    psum x1, waiting for transfers between devices, from_root(): return lax.psum(jnp.where(mine, x, jnp.zeros_like(x)), axis)  12.7 us
  transfers between devices with their start and end apart: 4, of which 4 were waited for; matrix products, arithmetic and copies ran while one was open for 2% of the time, Pallas kernels for 0%

commit v1 on v0

v1 whole, which is shorter than its diff:
```python
import functools
import math

import jax
import jax.numpy as jnp
from jax import lax
from jax.experimental import pallas as pl
from jax.experimental.pallas import tpu as pltpu
from jax.sharding import PartitionSpec as P

SPIN_SITES = 4096
HIDDEN_UNITS = 8192
PANEL_ROWS = 1024
SAMPLES = 4096
Z, Y, X, C = 8, 4, 4, 2
Q = X * C
NEAR = (0, 1, 7, 2, 6, 3, 5, 4)
FAR = (4, 3, 5, 2, 6, 1, 7, 0)
SAME = (2, 6, 4)
MESH = pl.DeviceIdType.MESH
BF = jnp.bfloat16
F32 = jnp.float32
CONTRACT = (((1,), (1,)), ((), ()))


class Sems:
    def __init__(self):
        self.n = 0

    def take(self, n):
        self.n += n
        return self.n - n


def layout():
    s = Sems()
    names = dict(
        wz=8, wy=24, sz=3, sx=9, sc=12, ez=8, ey=4, ps=7, pf=7,
        gc=2, gx=8, gz=8, uq=8, uz=4, r1=8, r2=16, r3=8,
    )
    return {k: s.take(n) for k, n in names.items()}, s.n


SEM, NSEM = layout()


def kernel(
    spins, weights, bias, energy, panel, diag,
    grad_out, factor_out, update_out,
    s32, sp, wg, dg, f5, ft, eg, psp, pf,
    gsend, gkeep, grecv, xsend, xrecv, tsum, zsend, zrecv,
    u1, u2, wt, pb, r1, qb, r2, zb, r3,
    ssem, rsem, lsem,
):
    wide = lax.axis_index("wide")
    q = lax.axis_index("narrow")
    z, y = wide // Y, wide % Y
    x, c = q // C, q % C
    par, j = z % 2, z // 2
    sib = x * C + (1 - c)
    sends = []

    def at_z(zz):
        return (zz * Y + y, q)

    def at_y(k):
        return (z * Y + (y + k) % Y, q)

    def at_x(k):
        return (wide, ((x + k) % X) * C + c)

    def send(src, dst, index, device):
        copy = pltpu.make_async_remote_copy(
            src_ref=src, dst_ref=dst, send_sem=ssem.at[index], recv_sem=rsem.at[index],
            device_id=device, device_id_type=MESH,
        )
        copy.start()
        sends.append(copy)

    def arrived(dst, index):
        pltpu.make_async_remote_copy(
            src_ref=dst, dst_ref=dst, send_sem=ssem.at[index], recv_sem=rsem.at[index],
            device_id=(wide, sib), device_id_type=MESH,
        ).wait_recv()

    def load_spins(k):
        return pltpu.make_async_copy(spins.at[:, pl.ds(pl.multiple_of(k * 512, 512), 512)], s32.at[k], lsem.at[k])

    for d in range(Q):
        load_spins((q + d) % Q).start()
    my_w = weights.at[:, pl.ds(pl.multiple_of(j * 256, 256), 256)]
    load_w = pltpu.make_async_copy(my_w, wg.at[wide], lsem.at[8])
    load_w.start()
    load_d = pltpu.make_async_copy(diag, dg, lsem.at[9])
    load_d.start()

    barrier = pltpu.get_barrier_semaphore()
    for d in range(1, Z):
        pl.semaphore_signal(barrier, inc=1, device_id=at_z((z + d) % Z), device_id_type=MESH)
    for k in range(1, Y):
        pl.semaphore_signal(barrier, inc=1, device_id=at_y(k), device_id_type=MESH)
    for d in range(1, Q):
        pl.semaphore_signal(barrier, inc=1, device_id=(wide, (q + d) % Q), device_id_type=MESH)

    def convert(k):
        load_spins(k).wait()
        sp[k, j] = s32[k].astype(F32).astype(BF)

    convert(q)
    eg[y, z] = energy[...]
    load_w.wait()
    pl.semaphore_wait(barrier, Z + Y + Q - 3)

    def w_y(i, z1):
        chunk = wg.at[z1 * Y + y]
        send(chunk, chunk, SEM["wy"] + i, at_y(1))
        send(chunk, chunk, SEM["wy"] + 8 + i, at_y(-1 + Y))

    def w_z(off):
        zd = (z + off) % Z
        src = weights.at[:, pl.ds(pl.multiple_of((zd // 2) * 256, 256), 256)]
        send(src, wg.at[wide], SEM["wz"] + off, at_z(zd))

    def s_z(t):
        send(sp.at[q, j], sp.at[q, j], SEM["sz"] + t, at_z((z + SAME[t]) % Z))

    w_y(0, z)
    w_z(1)
    w_z(7)
    s_z(0)
    s_z(1)
    w_z(2)
    w_z(6)
    s_z(2)
    w_z(3)
    w_z(5)
    w_z(4)
    for d in range(1, Z):
        send(eg.at[y, z], eg.at[y, z], SEM["ez"] + d, at_z((z + d) % Z))
    for d in range(1, Q):
        convert((q + d) % Q)

    def w_take(i):
        z1 = (z + NEAR[i]) % Z
        arrived(wg.at[z1 * Y + y], SEM["wz"] + (Z - NEAR[i]) % Z)
        w_y(i, z1)

    def w_relay(i):
        z1 = (z + NEAR[i]) % Z
        if i % 2 == 0:
            chunk = wg.at[z1 * Y + (y + 3) % Y]
            arrived(chunk, SEM["wy"] + i)
            send(chunk, chunk, SEM["wy"] + 16 + i, at_y(1))
        else:
            chunk = wg.at[z1 * Y + (y + 1) % Y]
            arrived(chunk, SEM["wy"] + 8 + i)
            send(chunk, chunk, SEM["wy"] + 16 + i, at_y(3))

    def zi_of(t):
        return ((z + SAME[t]) % Z) // 2

    sx, sc = SEM["sx"], SEM["sc"]

    def s_take(t):
        piece = sp.at[q, zi_of(t)]
        arrived(piece, SEM["sz"] + (1, 0, 2)[t])
        send(piece, piece, sx + t, at_x(1))
        send(piece, piece, sx + 3 + t, at_x(3))
        if t == 2:
            send(piece, piece, sx + 6 + t, at_x(2))
        send(piece, piece, sc + t, (wide, sib))

    def s_cross(t, k):
        source = ((x + (3, 1, 2)[k]) % X) * C + c
        piece = sp.at[source, zi_of(t)]
        arrived(piece, sx + 3 * k + t)
        if t == 0 and k == 0:
            send(piece, piece, sx + 6 + t, at_x(1))
        if t == 1 and k == 1:
            send(piece, piece, sx + 6 + t, at_x(3))
        send(piece, piece, sc + 3 * (k + 1) + t, (wide, sib))

    p = panel[0]
    slot = par * 4 + y
    other = (1 - par) * 4 + y
    partner = z + 1 - 2 * par

    def panel_send(buf, base):
        send(buf.at[slot], buf.at[slot], base, at_z(partner))
        for k in (1, 3, 2):
            send(buf.at[slot], buf.at[slot], base + k, at_y(k))

    def panel_pass(buf, base):
        arrived(buf.at[other], base)
        for k in (1, 3, 2):
            send(buf.at[other], buf.at[other], base + 3 + k, at_y(k))

    def panel_wait(buf, base):
        for k in (1, 3, 2):
            arrived(buf.at[par * 4 + (y + 4 - k) % 4], base + k)
            arrived(buf.at[(1 - par) * 4 + (y + 4 - k) % 4], base + 3 + k)

    sub = pl.ds(pl.multiple_of(j * 128, 128), 128)

    w_take(1)
    w_take(2)
    s_take(0)
    s_take(1)
    w_take(3)
    w_take(4)
    w_relay(0)
    w_relay(1)
    s_take(2)
    chosen = sp[q, 0, :, sub].astype(F32)
    for zi in range(1, 4):
        chosen = jnp.where(p == zi, sp[q, zi, :, sub].astype(F32), chosen)
    psp[slot] = chosen.astype(BF)
    panel_send(psp, SEM["ps"])
    w_take(5)
    w_take(6)
    w_relay(2)
    w_relay(3)
    s_cross(0, 0)
    s_cross(0, 1)
    s_cross(1, 0)
    s_cross(1, 1)
    w_take(7)
    for d in range(1, Z):
        arrived(eg.at[y, (z + d) % Z], SEM["ez"] + Z - d)
    for k in range(1, Y):
        send(eg.at[y], eg.at[y], SEM["ey"] + k, at_y(k))
    w_relay(4)
    w_relay(5)
    panel_pass(psp, SEM["ps"])
    s_cross(0, 2)
    s_cross(1, 2)
    s_cross(2, 0)
    s_cross(2, 1)
    s_cross(2, 2)
    w_relay(6)
    w_relay(7)

    panel_wait(psp, SEM["ps"])

    def gram_start(g, rows_of, panel_rows):
        rhs = panel_rows
        theirs = lax.dot_general(rows_of(1 - c), rhs, CONTRACT, preferred_element_type=F32)
        gsend[g] = theirs.astype(BF)
        send(gsend.at[g], grecv.at[g], SEM["gc"] + g, (wide, sib))
        gkeep[g] = lax.dot_general(rows_of(c), rhs, CONTRACT, preferred_element_type=F32)

    def spin_rows(cc):
        return jnp.concatenate(
            [
                sp[q, zi, pl.ds(pl.multiple_of((2 * xx + cc) * 16, 16), 16), sub]
                for xx in range(X)
                for zi in range(4)
            ],
            axis=0,
        )

    gram_start(0, spin_rows, psp[...].reshape(PANEL_ROWS, 128))

    for k in range(1, Y):
        arrived(eg.at[(y + 4 - k) % 4], SEM["ey"] + k)
    mean = jnp.sum(jnp.sum(eg[...].reshape(32, 128), axis=0, keepdims=True), axis=1, keepdims=True) / SAMPLES
    shifted = jnp.concatenate([eg[yy, 2 * p + zp] for zp in range(2) for yy in range(Y)], axis=1) - mean
    high = shifted.astype(BF).astype(F32)
    rest = shifted - high
    middle = rest.astype(BF).astype(F32)
    low = rest - middle
    row = lax.broadcasted_iota(jnp.int32, (16, PANEL_ROWS), 0)
    pieces = jnp.where(row == 0, high, jnp.where(row == 1, middle, jnp.where(row == 2, low, 0.0)))
    load_d.wait()
    solved = jnp.sum(
        lax.dot_general(pieces.astype(BF), dg[...], CONTRACT, preferred_element_type=F32), axis=0, keepdims=True
    )

    for t in range(3):
        for k in range(4):
            source = ((x + (0, 3, 1, 2)[k]) % X) * C + (1 - c)
            arrived(sp.at[source, zi_of(t)], sc + 3 * k + t)
    total = None
    for i in range(Z):
        z1 = (z + NEAR[i]) % Z
        if i % 2 == 0:
            arrived(wg.at[z1 * Y + (y + 1) % Y], SEM["wy"] + 8 + i)
        else:
            arrived(wg.at[z1 * Y + (y + 3) % Y], SEM["wy"] + i)
        arrived(wg.at[z1 * Y + (y + 2) % Y], SEM["wy"] + 16 + i)
        term = jnp.dot(
            sp[z1].reshape(512, 512), wg[pl.ds(z1 * Y, Y)].reshape(512, 256), preferred_element_type=F32
        )
        total = term if total is None else total + term
    mine = bias[:, pl.ds(pl.multiple_of(j * 256, 256), 256)]
    fields = jnp.tanh(total + mine).astype(BF)
    f5[...] = fields.reshape(4, X, C, 16, 256)
    pf[slot] = f5[p].reshape(128, 256)
    panel_send(pf, SEM["pf"])
    ft[...] = fields.astype(F32).T

    def gram_x(g):
        arrived(grecv.at[g], SEM["gc"] + g)
        for k in (1, 3, 2):
            rows = pl.ds(pl.multiple_of(((x + k) % X) * 64, 64), 64)
            xsend[g, k] = (gkeep[g, rows, :] + grecv[g, rows, :].astype(F32)).astype(BF)
            send(xsend.at[g, k], xrecv.at[g, k], SEM["gx"] + 4 * g + k, at_x(k))

    def gram_z(g):
        rows = pl.ds(pl.multiple_of(x * 64, 64), 64)
        value = gkeep[g, rows, :] + grecv[g, rows, :].astype(F32)
        for k in (1, 3, 2):
            arrived(xrecv.at[g, k], SEM["gx"] + 4 * g + k)
            value = value + xrecv[g, k].astype(F32)
        tsum[g] = value.reshape(4, 16, PANEL_ROWS)
        for k in (1, 3, 2):
            zi = (j + k) % 4
            zsend[g, k] = tsum[g, zi].astype(BF)
            send(zsend.at[g, k], zrecv.at[g, k], SEM["gz"] + 4 * g + k, at_z(2 * zi + par))

    def gram_end(g):
        value = tsum[g, j]
        for k in (1, 3, 2):
            arrived(zrecv.at[g, k], SEM["gz"] + 4 * g + k)
            value = value + zrecv[g, k].astype(F32)
        return value

    gram_x(0)
    panel_pass(pf, SEM["pf"])
    gram_z(0)
    panel_wait(pf, SEM["pf"])

    def field_rows(cc):
        return jnp.concatenate([f5[zi, xx, cc] for xx in range(X) for zi in range(4)], axis=0)

    gram_start(1, field_rows, pf[...].reshape(PANEL_ROWS, 256))
    gram_x(1)
    spin_total = gram_end(0)
    gram_z(1)
    field_total = gram_end(1)
    gram_column = (spin_total / SPIN_SITES * (field_total / HIDDEN_UNITS)).astype(BF)
    factor = lax.dot_general(gram_column, dg[...], CONTRACT, preferred_element_type=F32)
    factor_out[...] = factor.astype(BF)

    sample = lax.broadcasted_iota(jnp.int32, (16, PANEL_ROWS), 0)
    column = lax.broadcasted_iota(jnp.int32, (16, PANEL_ROWS), 1)
    picked = jnp.sum(
        jnp.where(column == slot * 128 + q * 16 + sample, solved, 0.0), axis=1, keepdims=True
    )
    carried = jnp.sum(factor * solved, axis=1, keepdims=True)
    narrow_row = lax.broadcasted_iota(jnp.int32, (16, 128), 0)
    narrow_col = lax.broadcasted_iota(jnp.int32, (16, 128), 1)
    here = narrow_col == q * 16 + narrow_row
    own = jnp.sum(jnp.where(here, energy[...], 0.0), axis=1, keepdims=True)
    in_panel = jnp.broadcast_to(p, (16, 1)) == j
    update = jnp.where(in_panel, picked, own - mean - carried)
    update_out[...] = jnp.sum(
        jnp.where(narrow_row == narrow_col, update, 0.0), axis=0, keepdims=True
    )
    u1[q] = jnp.sum(jnp.where(here, update, 0.0), axis=0, keepdims=True)
    for d in range(1, Q):
        send(u1.at[q], u1.at[q], SEM["uq"] + d, (wide, (q + d) % Q))
    for d in range(1, Q):
        arrived(u1.at[(q + Q - d) % Q], SEM["uq"] + d)
    u2[j] = jnp.sum(u1[...].reshape(Q, 128), axis=0, keepdims=True)
    for k in (1, 3, 2):
        send(u2.at[j], u2.at[j], SEM["uz"] + k, at_z(2 * ((j + k) % 4) + par))
    for k in (1, 3, 2):
        arrived(u2.at[(j + 4 - k) % 4], SEM["uz"] + k)
    coefficient = jnp.concatenate([u2[zi] for zi in range(4)], axis=1)
    wt[...] = (ft[...] * coefficient).astype(BF)

    def plain(i):
        if i % 2 == 0:
            send(pb.at[i, (y + 3) % Y], r2.at[1, i], SEM["r2"] + 8 + i, at_y(3))
        else:
            send(pb.at[i, (y + 1) % Y], r2.at[0, i], SEM["r2"] + i, at_y(1))

    def combine(i):
        arrived(r1.at[i], SEM["r1"] + i)
        k = 1 if i % 2 == 0 else 3
        qb[i] = (pb[i, (y + k) % Y].astype(F32) + r1[i].astype(F32)).astype(BF)
        if i % 2 == 0:
            send(qb.at[i], r2.at[0, i], SEM["r2"] + i, at_y(1))
        else:
            send(qb.at[i], r2.at[1, i], SEM["r2"] + 8 + i, at_y(3))

    def finish(i):
        z1 = (z + FAR[i]) % Z
        arrived(r2.at[0, i], SEM["r2"] + i)
        arrived(r2.at[1, i], SEM["r2"] + 8 + i)
        value = (pb[i, y].astype(F32) + r2[0, i].astype(F32) + r2[1, i].astype(F32)).astype(BF)
        if FAR[i] == 0:
            r3[z] = value
        else:
            zb[i] = value
            send(zb.at[i], r3.at[z], SEM["r3"] + FAR[i], at_z(z1))

    for i in range(Z):
        z1 = (z + FAR[i]) % Z
        product = jnp.dot(wt[...], sp[z1].reshape(512, 512), preferred_element_type=F32).astype(BF)
        for yy in range(Y):
            pb[i, yy] = product[:, yy * 128 : (yy + 1) * 128]
        send(pb.at[i, (y + 2) % Y], r1.at[i], SEM["r1"] + i, at_y(1 if i % 2 == 0 else 3))
        if i >= 2:
            plain(i - 2)
        if i >= 4:
            combine(i - 4)
    plain(6)
    plain(7)
    for i in range(4, Z):
        combine(i)
        finish(i - 4)
    for i in range(4, Z):
        finish(i)
    for d in range(1, Z):
        arrived(r3.at[(z + d) % Z], SEM["r3"] + Z - d)
    for jj in range(4):
        block = r3[2 * jj].astype(F32) + r3[2 * jj + 1].astype(F32)
        grad_out[:, jj * 256 : (jj + 1) * 256] = block.T / math.sqrt(SAMPLES)
    for copy in sends:
        copy.wait_send()


def local(spins, weights, field_bias, energies, panel_index, diag_inverse):
    vmem = pl.BlockSpec(memory_space=pltpu.VMEM)
    anywhere = pl.BlockSpec(memory_space=pl.ANY)
    smem = pl.BlockSpec(memory_space=pltpu.SMEM)
    grad_w, factor, update = pl.pallas_call(
        kernel,
        out_shape=(
            jax.ShapeDtypeStruct((128, 1024), F32),
            jax.ShapeDtypeStruct((16, PANEL_ROWS), BF),
            jax.ShapeDtypeStruct((1, 128), F32),
        ),
        in_specs=[anywhere, anywhere, vmem, vmem, smem, anywhere],
        out_specs=(vmem, vmem, vmem),
        scratch_shapes=[
            pltpu.VMEM((Q, 128, 512), jnp.int32),
            pltpu.VMEM((Q, 4, 128, 512), BF),
            pltpu.VMEM((32, 128, 256), BF),
            pltpu.VMEM((PANEL_ROWS, PANEL_ROWS), BF),
            pltpu.VMEM((4, X, C, 16, 256), BF),
            pltpu.VMEM((256, 512), F32),
            pltpu.VMEM((Y, Z, 1, 128), F32),
            pltpu.VMEM((8, 128, 128), BF),
            pltpu.VMEM((8, 128, 256), BF),
            pltpu.VMEM((2, 256, PANEL_ROWS), BF),
            pltpu.VMEM((2, 256, PANEL_ROWS), F32),
            pltpu.VMEM((2, 256, PANEL_ROWS), BF),
            pltpu.VMEM((2, 4, 64, PANEL_ROWS), BF),
            pltpu.VMEM((2, 4, 64, PANEL_ROWS), BF),
            pltpu.VMEM((2, 4, 16, PANEL_ROWS), F32),
            pltpu.VMEM((2, 4, 16, PANEL_ROWS), BF),
            pltpu.VMEM((2, 4, 16, PANEL_ROWS), BF),
            pltpu.VMEM((Q, 1, 128), F32),
            pltpu.VMEM((4, 1, 128), F32),
            pltpu.VMEM((256, 512), BF),
            pltpu.VMEM((Z, Y, 256, 128), BF),
            pltpu.VMEM((Z, 256, 128), BF),
            pltpu.VMEM((Z, 256, 128), BF),
            pltpu.VMEM((2, Z, 256, 128), BF),
            pltpu.VMEM((Z, 256, 128), BF),
            pltpu.VMEM((Z, 256, 128), BF),
            pltpu.SemaphoreType.DMA((NSEM,)),
            pltpu.SemaphoreType.DMA((NSEM,)),
            pltpu.SemaphoreType.DMA((10,)),
        ],
        compiler_params=pltpu.CompilerParams(
            collective_id=0, has_side_effects=True, vmem_limit_bytes=56 * 1024 * 1024
        ),
    )(
        spins,
        weights,
        field_bias.reshape(1, -1),
        energies.astype(F32).reshape(1, -1),
        panel_index,
        diag_inverse,
    )
    return grad_w, factor, update[0, :16]


def solution(mesh):
    in_specs = (P("wide", None), P("wide", "narrow"), P("narrow"), P("wide"), P(), P())
    out_specs = (P("wide", "narrow"), P(("wide", "narrow"), None), P(("wide", "narrow")))
    return jax.shard_map(local, mesh=mesh, in_specs=in_specs, out_specs=out_specs, check_vma=False)
```

time: 611 us -> 116 us (0.19)
  waiting for transfers between devices: 402 us -> 0 us
  blocking collectives: 142 us -> 0 us
  Pallas kernels: 0 us -> 108 us
  local copies, waits for them, and re-layouts: 28.4 us -> 4.4 us
  matrix products: 18.7 us -> 0 us
  between operations: 15.4 us -> 1.29 us
    unnamed x5 -> x0, waiting for transfers between devices: 229 us -> none
    psum x2 -> x0, blocking collectives: 142 us -> none  [the longest x1 72 us: local(): lax.psum(jnp.sum(energies.astype(jnp.float32)), 'wide') / total_samples]
    pallas_call x0 -> x1, Pallas kernels: none -> 108 us  [local(): pl.pallas_call(kernel, out_shape=(jax.ShapeDtypeStruct((128, 1024), F32),...]
    all_gather x1 -> x0, waiting for transfers between devices: 101 us -> none  [local(): lax.all_gather(weights, 'wide', axis=0, tiled=True)]
    psum x2 -> x0, waiting for transfers between devices: 71.9 us -> none  [the longest x1 59.2 us: local(): lax.psum(field_gram.astype(jnp.bfloat16), 'narrow').astype(jnp.float32)]
    unnamed x48 -> x2, local copies, waits for them, and re-layouts: 24.3 us -> 3.26 us
    dot_general x7 -> x0, matrix products: 18.7 us -> none  [the longest x1 6.12 us: local(): jnp.dot(columns, lax.all_gather(weights, 'wide', axis=0, tiled=True), pre...]
  transfers between devices with their start and end apart: 4 -> 0, of which waited for: 4 -> 0; matrix products, arithmetic and copies ran while one was open for 2% -> 0% of each run, Pallas kernels for 0% -> 0%
where the time goes in v1:
time: 116 us; the launch traced here: 115 us
  Pallas kernels  108 us (93%)
  local copies, waits for them, and re-layouts  4.4 us (4%)
  between operations  1.29 us (1%)
  other arithmetic  1.17 us (1%)
    pallas_call x1, Pallas kernels, local(): pl.pallas_call(kernel, out_shape=(jax.ShapeDtypeStruct((128, 1024), F32),...  108 us
    unnamed x2, local copies, waits for them, and re-layouts  3.26 us

profile of v1, /device:TPU:2, one launch (start us, length us, event | category | flops | bytes accessed | tf_op | source)
XLA Modules:
  0.0 115.4 jit_solution(5951472231782172838)
XLA Ops:
  1.3 1.2 %bitcast_convert_fusion.energy = f32[1,128]{1,0:T(1,128)} fusion(bf16[128]{0:T(256)(128)(2,1)} %param.9), kind=kLoop, calls=%fused_computation | loop fusion | flops 128 | bytes 768 | tf_op jit(solution)/shard_map/reshape | solution.py:476
  2.4 108.5 %shard_map.85 = (f32[128,1024]{1,0:T(8,128)}, bf16[16,1024]{1,0:T(8,128)(2,1)}, f32[1,128]{1,0:T(1,128)}) custom-call(s32[128,4096]{1,0:T(8,128)} %spins.1, bf16[128,1024]{1,0:T(8,128)(2,1)} %weights.1, f32[1,1024]{1,0:T(1,128)} %bitcast.6, f32[1,128]{1,0:T(1,128)} %bitcast_convert_fusion.energy, s32[1]{0:T(128)S(6)} %copy.11.panel, bf16[1024,1024]{1,0:T(8,128)(2,1)} %diag.1), custom_call_target="tpu_custom_call" | custom-call | tf_op jit(solution)/shard_map/pallas_call | solution.py:429
  110.9 1.1 slice_bitcast_fusion
  112.1 1.9 %copy.12 = f32[128,1024]{1,0:T(8,128)} copy(f32[128,1024]{1,0:T(8,128)} %get-tuple-element.12) | data formatting | bytes 1048576
  114.0 1.4 %copy.13 = bf16[16,1024]{1,0:T(8,128)(2,1)} copy(bf16[16,1024]{1,0:T(8,128)(2,1)} %get-tuple-element.13) | data formatting | bytes 65536

commit v2 on v1

--- a/solution.py
+++ b/solution.py
@@ -14,9 +14,10 @@
 SAMPLES = 4096
 Z, Y, X, C = 8, 4, 4, 2
 Q = X * C
-NEAR = (0, 1, 7, 2, 6, 3, 5, 4)
+NEAR = (0, 1, -1, -2, 2, -3, 3, 4)
 FAR = (4, 3, 5, 2, 6, 1, 7, 0)
 SAME = (2, 6, 4)
+UNITS = ((0, 0), (1, 1), (0, 1), (1, 0), (2, 0), (2, 1))
 MESH = pl.DeviceIdType.MESH
 BF = jnp.bfloat16
 F32 = jnp.float32
@@ -35,8 +36,8 @@
 def layout():
     s = Sems()
     names = dict(
-        wz=8, wy=24, sz=3, sx=9, sc=12, ez=8, ey=4, ps=7, pf=7,
-        gc=2, gx=8, gz=8, uq=8, uz=4, r1=8, r2=16, r3=8,
+        wz=8, wy=24, sz=6, sx=18, sc=24, ty=4, tx=18, tc=24, ez=8, ey=4, ps=7, pf=7, fy=4,
+        gc=2, gx=8, gz=8, uq=8, up=16, r3=8,
     )
     return {k: s.take(n) for k, n in names.items()}, s.n
 
@@ -47,9 +48,9 @@
 def kernel(
     spins, weights, bias, energy, panel, diag,
     grad_out, factor_out, update_out,
-    s32, sp, wg, dg, f5, ft, eg, psp, pf,
+    s32, sp, wg, dg, f5, eg, psp, pf,
     gsend, gkeep, grecv, xsend, xrecv, tsum, zsend, zrecv,
-    u1, u2, wt, pb, r1, qb, r2, zb, r3,
+    u1, u2, wt, s2, fty, zb, r3,
     ssem, rsem, lsem,
 ):
     wide = lax.axis_index("wide")
@@ -58,6 +59,8 @@
     x, c = q // C, q % C
     par, j = z % 2, z // 2
     sib = x * C + (1 - c)
+    sign = 1 - 2 * par
+    partner = z + sign
     sends = []
 
     def at_z(zz):
@@ -116,37 +119,45 @@
         send(chunk, chunk, SEM["wy"] + i, at_y(1))
         send(chunk, chunk, SEM["wy"] + 8 + i, at_y(-1 + Y))
 
-    def w_z(off):
-        zd = (z + off) % Z
+    def toward(o):
+        return (z + sign * o + Z) % Z
+
+    def w_z(o):
+        zd = toward(o)
         src = weights.at[:, pl.ds(pl.multiple_of((zd // 2) * 256, 256), 256)]
-        send(src, wg.at[wide], SEM["wz"] + off, at_z(zd))
-
-    def s_z(t):
-        send(sp.at[q, j], sp.at[q, j], SEM["sz"] + t, at_z((z + SAME[t]) % Z))
+        seen = {1: 1, -1: -1, 2: -2, -3: -3}[o]
+        send(src, wg.at[wide], SEM["wz"] + 3 + seen, at_z(zd))
+
+    def s_z(u):
+        t, h = UNITS[u]
+        mine = sp.at[q, j, pl.ds(64 * h, 64)]
+        send(mine, mine, SEM["sz"] + u, at_z((z + (6, 2)[t]) % Z))
 
     w_y(0, z)
-    w_z(1)
-    w_z(7)
     s_z(0)
     s_z(1)
+    w_z(1)
+    w_z(-1)
+    s_z(2)
+    s_z(3)
     w_z(2)
-    w_z(6)
-    s_z(2)
-    w_z(3)
-    w_z(5)
-    w_z(4)
+    w_z(-3)
     for d in range(1, Z):
         send(eg.at[y, z], eg.at[y, z], SEM["ez"] + d, at_z((z + d) % Z))
     for d in range(1, Q):
         convert((q + d) % Q)
 
     def w_take(i):
-        z1 = (z + NEAR[i]) % Z
-        arrived(wg.at[z1 * Y + y], SEM["wz"] + (Z - NEAR[i]) % Z)
+        o = NEAR[i]
+        z1 = toward(o)
+        chunk = wg.at[z1 * Y + y]
+        arrived(chunk, SEM["wz"] + 3 + o)
+        if o < 0:
+            send(chunk, chunk, SEM["wz"] + 4 - o, at_z(partner))
         w_y(i, z1)
 
     def w_relay(i):
-        z1 = (z + NEAR[i]) % Z
+        z1 = toward(NEAR[i])
         if i % 2 == 0:
             chunk = wg.at[z1 * Y + (y + 3) % Y]
             arrived(chunk, SEM["wy"] + i)
@@ -159,31 +170,53 @@
     def zi_of(t):
         return ((z + SAME[t]) % Z) // 2
 
-    sx, sc = SEM["sx"], SEM["sc"]
-
-    def s_take(t):
-        piece = sp.at[q, zi_of(t)]
-        arrived(piece, SEM["sz"] + (1, 0, 2)[t])
-        send(piece, piece, sx + t, at_x(1))
-        send(piece, piece, sx + 3 + t, at_x(3))
-        if t == 2:
-            send(piece, piece, sx + 6 + t, at_x(2))
-        send(piece, piece, sc + t, (wide, sib))
-
-    def s_cross(t, k):
-        source = ((x + (3, 1, 2)[k]) % X) * C + c
-        piece = sp.at[source, zi_of(t)]
-        arrived(piece, sx + 3 * k + t)
-        if t == 0 and k == 0:
-            send(piece, piece, sx + 6 + t, at_x(1))
-        if t == 1 and k == 1:
-            send(piece, piece, sx + 6 + t, at_x(3))
-        send(piece, piece, sc + 3 * (k + 1) + t, (wide, sib))
+    def s_piece(source, u):
+        t, h = UNITS[u]
+        return sp.at[source, zi_of(t), pl.ds(64 * h, 64)]
+
+    def s_arrive(u):
+        got = s_piece(q, u)
+        arrived(got, SEM["sz"] + u)
+        if u < 2:
+            send(got, got, SEM["sz"] + 4 + u, at_z((z + (6, 2)[u]) % Z))
+
+    def spread(piece, bx, bc):
+        def begin(u):
+            mine = piece(q, u)
+            send(mine, mine, bx + u, at_x(1))
+            send(mine, mine, bx + 6 + u, at_x(3))
+            send(mine, mine, bc + u, (wide, sib))
+
+        def cross(u, k):
+            source = ((x + (3, 1, 2)[k]) % X) * C + c
+            got = piece(source, u)
+            arrived(got, bx + 6 * k + u)
+            if k == u % 2:
+                send(got, got, bx + 12 + u, at_x((1, 3)[k]))
+            send(got, got, bc + 6 * (k + 1) + u, (wide, sib))
+
+        def end(u):
+            for k in range(4):
+                source = ((x + (0, 3, 1, 2)[k]) % X) * C + (1 - c)
+                arrived(piece(source, u), bc + 6 * k + u)
+
+        return begin, cross, end
+
+    s_begin, s_cross, s_end = spread(s_piece, SEM["sx"], SEM["sc"])
+    t_begin, t_cross, t_end = spread(
+        lambda source, u: s2.at[source, (y + u // 2 + 1) % Y, pl.ds(2 * (u % 2), 2)], SEM["tx"], SEM["tc"]
+    )
+
+    def t_send(k):
+        columns = pl.ds(pl.multiple_of(((y + k) % Y) * 128, 128), 128)
+        send(sp.at[q, :, :, columns], s2.at[q, y], SEM["ty"] + k, at_y(k))
+
+    def t_arrive(t):
+        arrived(s2.at[q, (y + t + 1) % Y], SEM["ty"] + Y - 1 - t)
 
     p = panel[0]
     slot = par * 4 + y
     other = (1 - par) * 4 + y
-    partner = z + 1 - 2 * par
 
     def panel_send(buf, base):
         send(buf.at[slot], buf.at[slot], base, at_z(partner))
@@ -202,43 +235,63 @@
 
     sub = pl.ds(pl.multiple_of(j * 128, 128), 128)
 
+    s_arrive(0)
+    s_begin(0)
+    s_arrive(1)
+    s_begin(1)
     w_take(1)
     w_take(2)
-    s_take(0)
-    s_take(1)
+    s_arrive(2)
+    s_begin(2)
+    s_arrive(3)
+    s_begin(3)
+    w_relay(0)
+    s_cross(0, 0)
+    s_cross(0, 1)
+    s_cross(1, 0)
+    s_cross(1, 1)
     w_take(3)
-    w_take(4)
-    w_relay(0)
     w_relay(1)
-    s_take(2)
+    s_arrive(4)
+    s_begin(4)
+    s_arrive(5)
+    s_begin(5)
+    w_relay(2)
     chosen = sp[q, 0, :, sub].astype(F32)
     for zi in range(1, 4):
         chosen = jnp.where(p == zi, sp[q, zi, :, sub].astype(F32), chosen)
     psp[slot] = chosen.astype(BF)
     panel_send(psp, SEM["ps"])
+    s_cross(2, 0)
+    s_cross(2, 1)
+    s_cross(3, 0)
+    s_cross(3, 1)
+    w_take(4)
+    w_relay(3)
     w_take(5)
     w_take(6)
-    w_relay(2)
-    w_relay(3)
-    s_cross(0, 0)
-    s_cross(0, 1)
-    s_cross(1, 0)
-    s_cross(1, 1)
+    w_relay(4)
+    s_cross(0, 2)
+    s_cross(1, 2)
+    s_cross(2, 2)
+    s_cross(3, 2)
+    s_cross(4, 0)
+    s_cross(4, 1)
+    s_cross(5, 0)
+    s_cross(5, 1)
     w_take(7)
+    w_relay(5)
+    panel_pass(psp, SEM["ps"])
     for d in range(1, Z):
         arrived(eg.at[y, (z + d) % Z], SEM["ez"] + Z - d)
     for k in range(1, Y):
         send(eg.at[y], eg.at[y], SEM["ey"] + k, at_y(k))
-    w_relay(4)
-    w_relay(5)
-    panel_pass(psp, SEM["ps"])
-    s_cross(0, 2)
-    s_cross(1, 2)
-    s_cross(2, 0)
-    s_cross(2, 1)
-    s_cross(2, 2)
     w_relay(6)
     w_relay(7)
+    s_cross(4, 2)
+    s_cross(5, 2)
+    for k in (1, 3, 2):
+        t_send(k)
 
     panel_wait(psp, SEM["ps"])
 
@@ -276,13 +329,11 @@
         lax.dot_general(pieces.astype(BF), dg[...], CONTRACT, preferred_element_type=F32), axis=0, keepdims=True
     )
 
-    for t in range(3):
-        for k in range(4):
-            source = ((x + (0, 3, 1, 2)[k]) % X) * C + (1 - c)
-            arrived(sp.at[source, zi_of(t)], sc + 3 * k + t)
+    for u in range(6):
+        s_end(u)
     total = None
     for i in range(Z):
-        z1 = (z + NEAR[i]) % Z
+        z1 = toward(NEAR[i])
         if i % 2 == 0:
             arrived(wg.at[z1 * Y + (y + 1) % Y], SEM["wy"] + 8 + i)
         else:
@@ -297,7 +348,6 @@
     f5[...] = fields.reshape(4, X, C, 16, 256)
     pf[slot] = f5[p].reshape(128, 256)
     panel_send(pf, SEM["pf"])
-    ft[...] = fields.astype(F32).T
 
     def gram_x(g):
         arrived(grecv.at[g], SEM["gc"] + g)
@@ -326,7 +376,14 @@
         return value
 
     gram_x(0)
+    for t in (0, 2):
+        t_arrive(t)
+        t_begin(2 * t)
+        t_begin(2 * t + 1)
+    fty[y] = fields.astype(F32).T.astype(BF)
     panel_pass(pf, SEM["pf"])
+    send(fty.at[y], fty.at[y], SEM["fy"], at_y(1))
+    send(fty.at[y], fty.at[y], SEM["fy"] + 1, at_y(3))
     gram_z(0)
     panel_wait(pf, SEM["pf"])
 
@@ -335,8 +392,22 @@
 
     gram_start(1, field_rows, pf[...].reshape(PANEL_ROWS, 256))
     gram_x(1)
+    t_arrive(1)
+    t_begin(2)
+    t_begin(3)
+    for u in (0, 1, 4, 5):
+        t_cross(u, 0)
+        t_cross(u, 1)
+    gram_z(1)
+    for k in range(2):
+        passed = fty.at[(y + (3, 1)[k]) % Y]
+        arrived(passed, SEM["fy"] + k)
+        part = fty.at[(y + (3, 1)[k]) % Y, pl.ds(128 * k, 128)]
+        send(part, part, SEM["fy"] + 2 + k, at_y((1, 3)[k]))
     spin_total = gram_end(0)
-    gram_z(1)
+    for u in (2, 3):
+        t_cross(u, 0)
+        t_cross(u, 1)
     field_total = gram_end(1)
     gram_column = (spin_total / SPIN_SITES * (field_total / HIDDEN_UNITS)).astype(BF)
     factor = lax.dot_general(gram_column, dg[...], CONTRACT, preferred_element_type=F32)
@@ -362,57 +433,45 @@
         send(u1.at[q], u1.at[q], SEM["uq"] + d, (wide, (q + d) % Q))
     for d in range(1, Q):
         arrived(u1.at[(q + Q - d) % Q], SEM["uq"] + d)
-    u2[j] = jnp.sum(u1[...].reshape(Q, 128), axis=0, keepdims=True)
-    for k in (1, 3, 2):
-        send(u2.at[j], u2.at[j], SEM["uz"] + k, at_z(2 * ((j + k) % 4) + par))
-    for k in (1, 3, 2):
-        arrived(u2.at[(j + 4 - k) % 4], SEM["uz"] + k)
-    coefficient = jnp.concatenate([u2[zi] for zi in range(4)], axis=1)
-    wt[...] = (ft[...] * coefficient).astype(BF)
-
-    def plain(i):
-        if i % 2 == 0:
-            send(pb.at[i, (y + 3) % Y], r2.at[1, i], SEM["r2"] + 8 + i, at_y(3))
-        else:
-            send(pb.at[i, (y + 1) % Y], r2.at[0, i], SEM["r2"] + i, at_y(1))
-
-    def combine(i):
-        arrived(r1.at[i], SEM["r1"] + i)
-        k = 1 if i % 2 == 0 else 3
-        qb[i] = (pb[i, (y + k) % Y].astype(F32) + r1[i].astype(F32)).astype(BF)
-        if i % 2 == 0:
-            send(qb.at[i], r2.at[0, i], SEM["r2"] + i, at_y(1))
-        else:
-            send(qb.at[i], r2.at[1, i], SEM["r2"] + 8 + i, at_y(3))
-
-    def finish(i):
+    u2[y, j] = jnp.sum(u1[...].reshape(Q, 128), axis=0, keepdims=True)
+    plane = [(kz, ky) for kz in (0, 1, 3, 2) for ky in (0, 1, 3, 2)][1:]
+    for kz, ky in plane:
+        device = ((2 * ((j + kz) % 4) + par) * Y + (y + ky) % Y, q)
+        send(u2.at[y, j], u2.at[y, j], SEM["up"] + 4 * kz + ky, device)
+    for u in range(6):
+        t_cross(u, 2)
+    for u in range(6):
+        t_end(u)
+    for k in range(2):
+        arrived(fty.at[(y + 2) % Y, pl.ds(128 * k, 128)], SEM["fy"] + 2 + k)
+    for kz, ky in plane:
+        arrived(u2.at[(y + 4 - ky) % Y, (j + 4 - kz) % 4], SEM["up"] + 4 * kz + ky)
+    for yy in range(Y):
+        coefficient = jnp.concatenate([u2[yy, zi] for zi in range(4)], axis=1)
+        wt[yy] = (fty[yy].astype(F32) * coefficient).astype(BF)
+
+    mine_y = pl.ds(pl.multiple_of(y * 128, 128), 128)
+
+    def sites(i, k):
         z1 = (z + FAR[i]) % Z
-        arrived(r2.at[0, i], SEM["r2"] + i)
-        arrived(r2.at[1, i], SEM["r2"] + 8 + i)
-        value = (pb[i, y].astype(F32) + r2[0, i].astype(F32) + r2[1, i].astype(F32)).astype(BF)
-        if FAR[i] == 0:
-            r3[z] = value
-        else:
-            zb[i] = value
-            send(zb.at[i], r3.at[z], SEM["r3"] + FAR[i], at_z(z1))
-
-    for i in range(Z):
-        z1 = (z + FAR[i]) % Z
-        product = jnp.dot(wt[...], sp[z1].reshape(512, 512), preferred_element_type=F32).astype(BF)
-        for yy in range(Y):
-            pb[i, yy] = product[:, yy * 128 : (yy + 1) * 128]
-        send(pb.at[i, (y + 2) % Y], r1.at[i], SEM["r1"] + i, at_y(1 if i % 2 == 0 else 3))
-        if i >= 2:
-            plain(i - 2)
-        if i >= 4:
-            combine(i - 4)
-    plain(6)
-    plain(7)
-    for i in range(4, Z):
-        combine(i)
-        finish(i - 4)
-    for i in range(4, Z):
-        finish(i)
+        if k == 0:
+            return sp[z1, :, :, mine_y].reshape(512, 128)
+        return s2[z1, (y + k) % Y].reshape(512, 128)
+
+    for i in range(0, Z, 2):
+        product = None
+        for k in range(Y):
+            both = jnp.concatenate([sites(i, k), sites(i + 1, k)], axis=1)
+            term = jnp.dot(wt[(y + k) % Y], both, preferred_element_type=F32)
+            product = term if product is None else product + term
+        for n in range(2):
+            value = product[:, n * 128 : (n + 1) * 128].astype(BF)
+            off = FAR[i + n]
+            if off == 0:
+                r3[z] = value
+            else:
+                zb[i + n] = value
+                send(zb.at[i + n], r3.at[z], SEM["r3"] + off, at_z((z + off) % Z))
     for d in range(1, Z):
         arrived(r3.at[(z + d) % Z], SEM["r3"] + Z - d)
     for jj in range(4):
@@ -441,7 +500,6 @@
             pltpu.VMEM((32, 128, 256), BF),
             pltpu.VMEM((PANEL_ROWS, PANEL_ROWS), BF),
             pltpu.VMEM((4, X, C, 16, 256), BF),
-            pltpu.VMEM((256, 512), F32),
             pltpu.VMEM((Y, Z, 1, 128), F32),
             pltpu.VMEM((8, 128, 128), BF),
             pltpu.VMEM((8, 128, 256), BF),
@@ -454,12 +512,10 @@
             pltpu.VMEM((2, 4, 16, PANEL_ROWS), BF),
             pltpu.VMEM((2, 4, 16, PANEL_ROWS), BF),
             pltpu.VMEM((Q, 1, 128), F32),
-            pltpu.VMEM((4, 1, 128), F32),
-            pltpu.VMEM((256, 512), BF),
-            pltpu.VMEM((Z, Y, 256, 128), BF),
-            pltpu.VMEM((Z, 256, 128), BF),
-            pltpu.VMEM((Z, 256, 128), BF),
-            pltpu.VMEM((2, Z, 256, 128), BF),
+            pltpu.VMEM((Y, 4, 1, 128), F32),
+            pltpu.VMEM((Y, 256, 512), BF),
+            pltpu.VMEM((Q, Y, 4, 128, 128), BF),
+            pltpu.VMEM((Y, 256, 512), BF),
             pltpu.VMEM((Z, 256, 128), BF),
             pltpu.VMEM((Z, 256, 128), BF),
             pltpu.SemaphoreType.DMA((NSEM,)),

time: 116 us -> 105 us (0.905)
  Pallas kernels: 108 us -> 98.1 us
    pallas_call x1, Pallas kernels: 108 us -> 98.1 us  [local(): pl.pallas_call(kernel, out_shape=(jax.ShapeDtypeStruct((128, 1024), F32),...]
where the time goes in v2:
time: 105 us
  Pallas kernels  98.1 us (93%)
  local copies, waits for them, and re-layouts  4.4 us (4%)
  between operations  1.29 us (1%)
  other arithmetic  1.17 us (1%)
    pallas_call x1, Pallas kernels, local(): pl.pallas_call(kernel, out_shape=(jax.ShapeDtypeStruct((128, 1024), F32),...  98.1 us
    unnamed x2, local copies, waits for them, and re-layouts  3.26 us

profile of v2, /device:TPU:2, one launch (start us, length us, event | category | flops | bytes accessed | tf_op | source)
XLA Modules:
  0.0 104.9 jit_solution(2232341567095049900)
XLA Ops:
  1.3 1.2 %bitcast_convert_fusion.energy = f32[1,128]{1,0:T(1,128)} fusion(bf16[128]{0:T(256)(128)(2,1)} %param.9), kind=kLoop, calls=%fused_computation | loop fusion | flops 128 | bytes 768 | tf_op jit(solution)/shard_map/reshape | solution.py:532
  2.4 98.1 %shard_map.85 = (f32[128,1024]{1,0:T(8,128)}, bf16[16,1024]{1,0:T(8,128)(2,1)}, f32[1,128]{1,0:T(1,128)}) custom-call(s32[128,4096]{1,0:T(8,128)} %spins.1, bf16[128,1024]{1,0:T(8,128)(2,1)} %weights.1, f32[1,1024]{1,0:T(1,128)} %bitcast.6, f32[1,128]{1,0:T(1,128)} %bitcast_convert_fusion.energy, s32[1]{0:T(128)S(6)} %copy.11.panel, bf16[1024,1024]{1,0:T(8,128)(2,1)} %diag.1), custom_call_target="tpu_custom_call" | custom-call | tf_op jit(solution)/shard_map/pallas_call | solution.py:488
  100.5 1.1 %slice_bitcast_fusion = f32[16]{0:T(128)} fusion(f32[1,128]{1,0:T(1,128)} %get-tuple-element.8), kind=kLoop, calls=%fused_computation.1 | loop fusion | bytes 128 | tf_op jit(solution)/shard_map/squeeze | solution.py:536
  101.7 1.9 %copy.12 = f32[128,1024]{1,0:T(8,128)} copy(f32[128,1024]{1,0:T(8,128)} %get-tuple-element.12) | data formatting | bytes 1048576
  103.6 1.4 %copy.13 = bf16[16,1024]{1,0:T(8,128)(2,1)} copy(bf16[16,1024]{1,0:T(8,128)(2,1)} %get-tuple-element.13) | data formatting | bytes 65536

commit v3 on v2

--- a/solution.py
+++ b/solution.py
@@ -47,10 +47,10 @@
 
 def kernel(
     spins, weights, bias, energy, panel, diag,
-    grad_out, factor_out, update_out,
+    r3, factor_out, update_out,
     s32, sp, wg, dg, f5, eg, psp, pf,
     gsend, gkeep, grecv, xsend, xrecv, tsum, zsend, zrecv,
-    u1, u2, wt, s2, fty, zb, r3,
+    u1, u2, wt, s2, fty, zb,
     ssem, rsem, lsem,
 ):
     wide = lax.axis_index("wide")
@@ -110,7 +110,8 @@
         sp[k, j] = s32[k].astype(F32).astype(BF)
 
     convert(q)
-    eg[y, z] = energy[...]
+    energy_row = energy[...].astype(F32).reshape(1, 128)
+    eg[y, z] = energy_row
     load_w.wait()
     pl.semaphore_wait(barrier, Z + Y + Q - 3)
 
@@ -290,10 +291,6 @@
     w_relay(7)
     s_cross(4, 2)
     s_cross(5, 2)
-    for k in (1, 3, 2):
-        t_send(k)
-
-    panel_wait(psp, SEM["ps"])
 
     def gram_start(g, rows_of, panel_rows):
         rhs = panel_rows
@@ -312,22 +309,34 @@
             axis=0,
         )
 
-    gram_start(0, spin_rows, psp[...].reshape(PANEL_ROWS, 128))
-
-    for k in range(1, Y):
-        arrived(eg.at[(y + 4 - k) % 4], SEM["ey"] + k)
-    mean = jnp.sum(jnp.sum(eg[...].reshape(32, 128), axis=0, keepdims=True), axis=1, keepdims=True) / SAMPLES
-    shifted = jnp.concatenate([eg[yy, 2 * p + zp] for zp in range(2) for yy in range(Y)], axis=1) - mean
-    high = shifted.astype(BF).astype(F32)
-    rest = shifted - high
-    middle = rest.astype(BF).astype(F32)
-    low = rest - middle
-    row = lax.broadcasted_iota(jnp.int32, (16, PANEL_ROWS), 0)
-    pieces = jnp.where(row == 0, high, jnp.where(row == 1, middle, jnp.where(row == 2, low, 0.0)))
-    load_d.wait()
-    solved = jnp.sum(
-        lax.dot_general(pieces.astype(BF), dg[...], CONTRACT, preferred_element_type=F32), axis=0, keepdims=True
-    )
+    def gram_x(g):
+        arrived(grecv.at[g], SEM["gc"] + g)
+        for k in (1, 3, 2):
+            rows = pl.ds(pl.multiple_of(((x + k) % X) * 64, 64), 64)
+            xsend[g, k] = (gkeep[g, rows, :] + grecv[g, rows, :].astype(F32)).astype(BF)
+            send(xsend.at[g, k], xrecv.at[g, k], SEM["gx"] + 4 * g + k, at_x(k))
+
+    def gram_z(g):
+        rows = pl.ds(pl.multiple_of(x * 64, 64), 64)
+        value = gkeep[g, rows, :] + grecv[g, rows, :].astype(F32)
+        for k in (1, 3, 2):
+            arrived(xrecv.at[g, k], SEM["gx"] + 4 * g + k)
+            value = value + xrecv[g, k].astype(F32)
+        tsum[g] = value.reshape(4, 16, PANEL_ROWS)
+        for k in (1, 3, 2):
+            zi = (j + k) % 4
+            zsend[g, k] = tsum[g, zi].astype(BF)
+            send(zsend.at[g, k], zrecv.at[g, k], SEM["gz"] + 4 * g + k, at_z(2 * zi + par))
+
+    def gram_end(g):
+        value = tsum[g, j]
+        for k in (1, 3, 2):
+            arrived(zrecv.at[g, k], SEM["gz"] + 4 * g + k)
+            value = value + zrecv[g, k].astype(F32)
+        return value
+
+    def field_rows(cc):
+        return jnp.concatenate([f5[zi, xx, cc] for xx in range(X) for zi in range(4)], axis=0)
 
     for u in range(6):
         s_end(u)
@@ -349,55 +358,37 @@
     pf[slot] = f5[p].reshape(128, 256)
     panel_send(pf, SEM["pf"])
 
-    def gram_x(g):
-        arrived(grecv.at[g], SEM["gc"] + g)
-        for k in (1, 3, 2):
-            rows = pl.ds(pl.multiple_of(((x + k) % X) * 64, 64), 64)
-            xsend[g, k] = (gkeep[g, rows, :] + grecv[g, rows, :].astype(F32)).astype(BF)
-            send(xsend.at[g, k], xrecv.at[g, k], SEM["gx"] + 4 * g + k, at_x(k))
-
-    def gram_z(g):
-        rows = pl.ds(pl.multiple_of(x * 64, 64), 64)
-        value = gkeep[g, rows, :] + grecv[g, rows, :].astype(F32)
-        for k in (1, 3, 2):
-            arrived(xrecv.at[g, k], SEM["gx"] + 4 * g + k)
-            value = value + xrecv[g, k].astype(F32)
-        tsum[g] = value.reshape(4, 16, PANEL_ROWS)
-        for k in (1, 3, 2):
-            zi = (j + k) % 4
-            zsend[g, k] = tsum[g, zi].astype(BF)
-            send(zsend.at[g, k], zrecv.at[g, k], SEM["gz"] + 4 * g + k, at_z(2 * zi + par))
-
-    def gram_end(g):
-        value = tsum[g, j]
-        for k in (1, 3, 2):
-            arrived(zrecv.at[g, k], SEM["gz"] + 4 * g + k)
-            value = value + zrecv[g, k].astype(F32)
-        return value
-
+    panel_wait(psp, SEM["ps"])
+    gram_start(0, spin_rows, psp[...].reshape(PANEL_ROWS, 128))
+    panel_pass(pf, SEM["pf"])
+    for k in (1, 3, 2):
+        t_send(k)
+    fty[y] = fields.astype(F32).T.astype(BF)
+    send(fty.at[y], fty.at[y], SEM["fy"], at_y(1))
+    send(fty.at[y], fty.at[y], SEM["fy"] + 1, at_y(3))
     gram_x(0)
-    for t in (0, 2):
+    for k in range(1, Y):
+        arrived(eg.at[(y + 4 - k) % 4], SEM["ey"] + k)
+    mean = jnp.sum(jnp.sum(eg[...].reshape(32, 128), axis=0, keepdims=True), axis=1, keepdims=True) / SAMPLES
+    shifted = jnp.concatenate([eg[yy, 2 * p + zp] for zp in range(2) for yy in range(Y)], axis=1) - mean
+    high = shifted.astype(BF).astype(F32)
+    rest = shifted - high
+    middle = rest.astype(BF).astype(F32)
+    low = rest - middle
+    row = lax.broadcasted_iota(jnp.int32, (16, PANEL_ROWS), 0)
+    pieces = jnp.where(row == 0, high, jnp.where(row == 1, middle, jnp.where(row == 2, low, 0.0)))
+    load_d.wait()
+    solved = jnp.sum(
+        lax.dot_general(pieces.astype(BF), dg[...], CONTRACT, preferred_element_type=F32), axis=0, keepdims=True
+    )
+    panel_wait(pf, SEM["pf"])
+    gram_start(1, field_rows, pf[...].reshape(PANEL_ROWS, 256))
+    gram_x(1)
+    gram_z(0)
+    for t in (0, 2, 1):
         t_arrive(t)
         t_begin(2 * t)
         t_begin(2 * t + 1)
-    fty[y] = fields.astype(F32).T.astype(BF)
-    panel_pass(pf, SEM["pf"])
-    send(fty.at[y], fty.at[y], SEM["fy"], at_y(1))
-    send(fty.at[y], fty.at[y], SEM["fy"] + 1, at_y(3))
-    gram_z(0)
-    panel_wait(pf, SEM["pf"])
-
-    def field_rows(cc):
-        return jnp.concatenate([f5[zi, xx, cc] for xx in range(X) for zi in range(4)], axis=0)
-
-    gram_start(1, field_rows, pf[...].reshape(PANEL_ROWS, 256))
-    gram_x(1)
-    t_arrive(1)
-    t_begin(2)
-    t_begin(3)
-    for u in (0, 1, 4, 5):
-        t_cross(u, 0)
-        t_cross(u, 1)
     gram_z(1)
     for k in range(2):
         passed = fty.at[(y + (3, 1)[k]) % Y]
@@ -405,7 +396,7 @@
         part = fty.at[(y + (3, 1)[k]) % Y, pl.ds(128 * k, 128)]
         send(part, part, SEM["fy"] + 2 + k, at_y((1, 3)[k]))
     spin_total = gram_end(0)
-    for u in (2, 3):
+    for u in (0, 1, 4, 5):
         t_cross(u, 0)
         t_cross(u, 1)
     field_total = gram_end(1)
@@ -422,7 +413,7 @@
     narrow_row = lax.broadcasted_iota(jnp.int32, (16, 128), 0)
     narrow_col = lax.broadcasted_iota(jnp.int32, (16, 128), 1)
     here = narrow_col == q * 16 + narrow_row
-    own = jnp.sum(jnp.where(here, energy[...], 0.0), axis=1, keepdims=True)
+    own = jnp.sum(jnp.where(here, energy_row, 0.0), axis=1, keepdims=True)
     in_panel = jnp.broadcast_to(p, (16, 1)) == j
     update = jnp.where(in_panel, picked, own - mean - carried)
     update_out[...] = jnp.sum(
@@ -431,6 +422,9 @@
     u1[q] = jnp.sum(jnp.where(here, update, 0.0), axis=0, keepdims=True)
     for d in range(1, Q):
         send(u1.at[q], u1.at[q], SEM["uq"] + d, (wide, (q + d) % Q))
+    for u in (2, 3):
+        t_cross(u, 0)
+        t_cross(u, 1)
     for d in range(1, Q):
         arrived(u1.at[(q + Q - d) % Q], SEM["uq"] + d)
     u2[y, j] = jnp.sum(u1[...].reshape(Q, 128), axis=0, keepdims=True)
@@ -474,21 +468,26 @@
                 send(zb.at[i + n], r3.at[z], SEM["r3"] + off, at_z((z + off) % Z))
     for d in range(1, Z):
         arrived(r3.at[(z + d) % Z], SEM["r3"] + Z - d)
-    for jj in range(4):
-        block = r3[2 * jj].astype(F32) + r3[2 * jj + 1].astype(F32)
-        grad_out[:, jj * 256 : (jj + 1) * 256] = block.T / math.sqrt(SAMPLES)
     for copy in sends:
         copy.wait_send()
+
+
+def finish(terms, factor, update, grad_out, factor_out, update_out):
+    factor_out[...] = factor[...]
+    update_out[...] = update[0, :16]
+    for jj in range(4):
+        block = terms[2 * jj].astype(F32) + terms[2 * jj + 1].astype(F32)
+        grad_out[:, jj * 256 : (jj + 1) * 256] = block.T / math.sqrt(SAMPLES)
 
 
 def local(spins, weights, field_bias, energies, panel_index, diag_inverse):
     vmem = pl.BlockSpec(memory_space=pltpu.VMEM)
     anywhere = pl.BlockSpec(memory_space=pl.ANY)
     smem = pl.BlockSpec(memory_space=pltpu.SMEM)
-    grad_w, factor, update = pl.pallas_call(
+    terms, factor, update = pl.pallas_call(
         kernel,
         out_shape=(
-            jax.ShapeDtypeStruct((128, 1024), F32),
+            jax.ShapeDtypeStruct((Z, 256, 128), BF),
             jax.ShapeDtypeStruct((16, PANEL_ROWS), BF),
             jax.ShapeDtypeStruct((1, 128), F32),
         ),
@@ -517,7 +516,6 @@
             pltpu.VMEM((Q, Y, 4, 128, 128), BF),
             pltpu.VMEM((Y, 256, 512), BF),
             pltpu.VMEM((Z, 256, 128), BF),
-            pltpu.VMEM((Z, 256, 128), BF),
             pltpu.SemaphoreType.DMA((NSEM,)),
             pltpu.SemaphoreType.DMA((NSEM,)),
             pltpu.SemaphoreType.DMA((10,)),
@@ -529,11 +527,20 @@
         spins,
         weights,
         field_bias.reshape(1, -1),
-        energies.astype(F32).reshape(1, -1),
+        energies,
         panel_index,
         diag_inverse,
     )
-    return grad_w, factor, update[0, :16]
+    return pl.pallas_call(
+        finish,
+        out_shape=(
+            jax.ShapeDtypeStruct((128, 1024), F32),
+            jax.ShapeDtypeStruct((16, PANEL_ROWS), BF),
+            jax.ShapeDtypeStruct((16,), F32),
+        ),
+        in_specs=[vmem, vmem, vmem],
+        out_specs=(vmem, vmem, vmem),
+    )(terms, factor, update)
 
 
 def solution(mesh):

time: 105 us -> 101 us (0.962)
  local copies, waits for them, and re-layouts: 4.4 us -> 0 us
  other arithmetic: 1.17 us -> 0 us
    unnamed x2 -> x0, local copies, waits for them, and re-layouts: 3.26 us -> none
    reshape x1 -> x0, other arithmetic: 1.17 us -> none  [local(): energies.astype(F32).reshape(1, -1)]
    squeeze x1 -> x0, local copies, waits for them, and re-layouts: 1.14 us -> none  [local(): return (grad_w, factor, update[0, :16])]
    pallas_call x1 -> x2, Pallas kernels: 98.1 us -> 98.9 us  [the longest x1 96.9 us: local(): pl.pallas_call(kernel, out_shape=(jax.ShapeDtypeStruct((Z, 256, 128), BF)...]
where the time goes in v3:
time: 101 us; the launch traced here: 100 us
  Pallas kernels  98.9 us (98%)
  between operations  1.29 us (1%)
    pallas_call x1, Pallas kernels, local(): pl.pallas_call(kernel, out_shape=(jax.ShapeDtypeStruct((Z, 256, 128), BF)...  96.9 us
    pallas_call x1, Pallas kernels, local(): pl.pallas_call(finish, out_shape=(jax.ShapeDtypeStruct((128, 1024), F32),...  2.07 us

profile of v3, /device:TPU:2, one launch (start us, length us, event | category | flops | bytes accessed | tf_op | source)
XLA Modules:
  0.0 100.2 jit_solution(15459714939956825698)
XLA Ops:
  1.3 96.9 %shard_map.85 = (bf16[8,256,128]{2,1,0:T(8,128)(2,1)}, bf16[16,1024]{1,0:T(8,128)(2,1)}, f32[1,128]{1,0:T(1,128)}) custom-call(s32[128,4096]{1,0:T(8,128)} %spins.1, bf16[128,1024]{1,0:T(8,128)(2,1)} %weights.1, f32[1,1024]{1,0:T(1,128)} %bitcast.1, bf16[128]{0:T(256)(128)(2,1)} %energy.1, s32[1]{0:T(128)S(6)} %copy.9.panel, bf16[1024,1024]{1,0:T(8,128)(2,1)} %diag.1), custom_call_target="tpu_custom_call" | custom-call | tf_op jit(solution)/shard_map/pallas_call | solution.py:487
  98.1 2.1 %shard_map.86 = (f32[128,1024]{1,0:T(8,128)}, bf16[16,1024]{1,0:T(8,128)(2,1)}, f32[16]{0:T(128)}) custom-call(bf16[8,256,128]{2,1,0:T(8,128)(2,1)} %get-tuple-element.6.terms, bf16[16,1024]{1,0:T(8,128)(2,1)} %get-tuple-element.7.factor, f32[1,128]{1,0:T(1,128)} %get-tuple-element.8.update), custom_call_target="tpu_custom_call" | custom-call | tf_op jit(solution)/shard_map/pallas_call | solution.py:534

commit v4 on v3

--- a/solution.py
+++ b/solution.py
@@ -15,8 +15,8 @@
 Z, Y, X, C = 8, 4, 4, 2
 Q = X * C
 NEAR = (0, 1, -1, -2, 2, -3, 3, 4)
-FAR = (4, 3, 5, 2, 6, 1, 7, 0)
 SAME = (2, 6, 4)
+GRAMS = ((0, 0, 1024), (1, 0, 512), (1, 512, 512))
 UNITS = ((0, 0), (1, 1), (0, 1), (1, 0), (2, 0), (2, 1))
 MESH = pl.DeviceIdType.MESH
 BF = jnp.bfloat16
@@ -37,7 +37,7 @@
     s = Sems()
     names = dict(
         wz=8, wy=24, sz=6, sx=18, sc=24, ty=4, tx=18, tc=24, ez=8, ey=4, ps=7, pf=7, fy=4,
-        gc=2, gx=8, gz=8, uq=8, up=16, r3=8,
+        gc=3, gx=12, gz=12, uq=8, up=16, r3=8, rel=2,
     )
     return {k: s.take(n) for k, n in names.items()}, s.n
 
@@ -49,8 +49,8 @@
     spins, weights, bias, energy, panel, diag,
     r3, factor_out, update_out,
     s32, sp, wg, dg, f5, eg, psp, pf,
-    gsend, gkeep, grecv, xsend, xrecv, tsum, zsend, zrecv,
-    u1, u2, wt, s2, fty, zb,
+    ftot, gsend, gkeep, grecv, xsend, xrecv, tsum, zsend, zrecv,
+    u1, u2, wt, s2, fty, zb, rel, nearsum,
     ssem, rsem, lsem,
 ):
     wide = lax.axis_index("wide")
@@ -147,6 +147,8 @@
         send(eg.at[y, z], eg.at[y, z], SEM["ez"] + d, at_z((z + d) % Z))
     for d in range(1, Q):
         convert((q + d) % Q)
+    for o in (3, 4):
+        r3[toward(o)] = jnp.zeros((256, 128), BF)
 
     def w_take(i):
         o = NEAR[i]
@@ -229,12 +231,71 @@
         for k in (1, 3, 2):
             send(buf.at[other], buf.at[other], base + 3 + k, at_y(k))
 
-    def panel_wait(buf, base):
+    def panel_wait(buf, base, half):
         for k in (1, 3, 2):
-            arrived(buf.at[par * 4 + (y + 4 - k) % 4], base + k)
-            arrived(buf.at[(1 - par) * 4 + (y + 4 - k) % 4], base + 3 + k)
+            group = (1 - par) if half else par
+            arrived(buf.at[group * 4 + (y + 4 - k) % 4], base + 3 * half + k)
 
     sub = pl.ds(pl.multiple_of(j * 128, 128), 128)
+
+    def gram_start(part, rows_of, rhs):
+        g, first, width = GRAMS[part]
+        columns = pl.ds(first, width)
+        theirs = lax.dot_general(rows_of(1 - c), rhs, CONTRACT, preferred_element_type=F32)
+        gsend[g, :, columns] = theirs.astype(BF)
+        send(gsend.at[g, :, columns], grecv.at[g, :, columns], SEM["gc"] + part, (wide, sib))
+        gkeep[g, :, columns] = lax.dot_general(rows_of(c), rhs, CONTRACT, preferred_element_type=F32)
+
+    def spin_rows(cc):
+        return jnp.concatenate(
+            [
+                sp[q, zi, pl.ds(pl.multiple_of((2 * xx + cc) * 16, 16), 16), sub]
+                for xx in range(X)
+                for zi in range(4)
+            ],
+            axis=0,
+        )
+
+    def gram_x(part):
+        g, first, width = GRAMS[part]
+        columns = pl.ds(first, width)
+        arrived(grecv.at[g, :, columns], SEM["gc"] + part)
+        for k in (2, 1, 3):
+            rows = pl.ds(pl.multiple_of(((x + k) % X) * 64, 64), 64)
+            value = gkeep[g, rows, columns] + grecv[g, rows, columns].astype(F32)
+            xsend[g, k, :, columns] = value.astype(BF)
+            send(xsend.at[g, k, :, columns], xrecv.at[g, k, :, columns], SEM["gx"] + 4 * part + k, at_x(k))
+
+    def gram_z(part):
+        g, first, width = GRAMS[part]
+        columns = pl.ds(first, width)
+        rows = pl.ds(pl.multiple_of(x * 64, 64), 64)
+        value = gkeep[g, rows, columns] + grecv[g, rows, columns].astype(F32)
+        for k in (1, 3, 2):
+            arrived(xrecv.at[g, k, :, columns], SEM["gx"] + 4 * part + k)
+            value = value + xrecv[g, k, :, columns].astype(F32)
+        tsum[g, :, :, columns] = value.reshape(4, 16, width)
+        for k in (2, 1, 3):
+            zi = (j + k) % 4
+            zsend[g, k, :, columns] = tsum[g, zi, :, columns].astype(BF)
+            send(
+                zsend.at[g, k, :, columns],
+                zrecv.at[g, k, :, columns],
+                SEM["gz"] + 4 * part + k,
+                at_z(2 * zi + par),
+            )
+
+    def gram_end(part):
+        g, first, width = GRAMS[part]
+        columns = pl.ds(first, width)
+        value = tsum[g, j, :, columns]
+        for k in (1, 3, 2):
+            arrived(zrecv.at[g, k, :, columns], SEM["gz"] + 4 * part + k)
+            value = value + zrecv[g, k, :, columns].astype(F32)
+        return value
+
+    def field_rows(cc):
+        return jnp.concatenate([f5[zi, xx, cc] for xx in range(X) for zi in range(4)], axis=0)
 
     s_arrive(0)
     s_begin(0)
@@ -276,67 +337,25 @@
     s_cross(1, 2)
     s_cross(2, 2)
     s_cross(3, 2)
+    panel_pass(psp, SEM["ps"])
     s_cross(4, 0)
     s_cross(4, 1)
     s_cross(5, 0)
     s_cross(5, 1)
     w_take(7)
     w_relay(5)
-    panel_pass(psp, SEM["ps"])
     for d in range(1, Z):
         arrived(eg.at[y, (z + d) % Z], SEM["ez"] + Z - d)
     for k in range(1, Y):
         send(eg.at[y], eg.at[y], SEM["ey"] + k, at_y(k))
     w_relay(6)
+    panel_wait(psp, SEM["ps"], 0)
+    panel_wait(psp, SEM["ps"], 1)
+    gram_start(0, spin_rows, psp[...].reshape(PANEL_ROWS, 128))
     w_relay(7)
     s_cross(4, 2)
     s_cross(5, 2)
-
-    def gram_start(g, rows_of, panel_rows):
-        rhs = panel_rows
-        theirs = lax.dot_general(rows_of(1 - c), rhs, CONTRACT, preferred_element_type=F32)
-        gsend[g] = theirs.astype(BF)
-        send(gsend.at[g], grecv.at[g], SEM["gc"] + g, (wide, sib))
-        gkeep[g] = lax.dot_general(rows_of(c), rhs, CONTRACT, preferred_element_type=F32)
-
-    def spin_rows(cc):
-        return jnp.concatenate(
-            [
-                sp[q, zi, pl.ds(pl.multiple_of((2 * xx + cc) * 16, 16), 16), sub]
-                for xx in range(X)
-                for zi in range(4)
-            ],
-            axis=0,
-        )
-
-    def gram_x(g):
-        arrived(grecv.at[g], SEM["gc"] + g)
-        for k in (1, 3, 2):
-            rows = pl.ds(pl.multiple_of(((x + k) % X) * 64, 64), 64)
-            xsend[g, k] = (gkeep[g, rows, :] + grecv[g, rows, :].astype(F32)).astype(BF)
-            send(xsend.at[g, k], xrecv.at[g, k], SEM["gx"] + 4 * g + k, at_x(k))
-
-    def gram_z(g):
-        rows = pl.ds(pl.multiple_of(x * 64, 64), 64)
-        value = gkeep[g, rows, :] + grecv[g, rows, :].astype(F32)
-        for k in (1, 3, 2):
-            arrived(xrecv.at[g, k], SEM["gx"] + 4 * g + k)
-            value = value + xrecv[g, k].astype(F32)
-        tsum[g] = value.reshape(4, 16, PANEL_ROWS)
-        for k in (1, 3, 2):
-            zi = (j + k) % 4
-            zsend[g, k] = tsum[g, zi].astype(BF)
-            send(zsend.at[g, k], zrecv.at[g, k], SEM["gz"] + 4 * g + k, at_z(2 * zi + par))
-
-    def gram_end(g):
-        value = tsum[g, j]
-        for k in (1, 3, 2):
-            arrived(zrecv.at[g, k], SEM["gz"] + 4 * g + k)
-            value = value + zrecv[g, k].astype(F32)
-        return value
-
-    def field_rows(cc):
-        return jnp.concatenate([f5[zi, xx, cc] for xx in range(X) for zi in range(4)], axis=0)
+    gram_x(0)
 
     for u in range(6):
         s_end(u)
@@ -358,15 +377,15 @@
     pf[slot] = f5[p].reshape(128, 256)
     panel_send(pf, SEM["pf"])
 
-    panel_wait(psp, SEM["ps"])
-    gram_start(0, spin_rows, psp[...].reshape(PANEL_ROWS, 128))
+    fty[y] = fields.astype(F32).T.astype(BF)
     panel_pass(pf, SEM["pf"])
     for k in (1, 3, 2):
         t_send(k)
-    fty[y] = fields.astype(F32).T.astype(BF)
     send(fty.at[y], fty.at[y], SEM["fy"], at_y(1))
     send(fty.at[y], fty.at[y], SEM["fy"] + 1, at_y(3))
-    gram_x(0)
+    panel_wait(pf, SEM["pf"], 0)
+    gram_start(1, field_rows, pf[pl.ds(par * 4, 4)].reshape(512, 256))
+    gram_x(1)
     for k in range(1, Y):
         arrived(eg.at[(y + 4 - k) % 4], SEM["ey"] + k)
     mean = jnp.sum(jnp.sum(eg[...].reshape(32, 128), axis=0, keepdims=True), axis=1, keepdims=True) / SAMPLES
@@ -381,25 +400,34 @@
     solved = jnp.sum(
         lax.dot_general(pieces.astype(BF), dg[...], CONTRACT, preferred_element_type=F32), axis=0, keepdims=True
     )
-    panel_wait(pf, SEM["pf"])
-    gram_start(1, field_rows, pf[...].reshape(PANEL_ROWS, 256))
-    gram_x(1)
+    panel_wait(pf, SEM["pf"], 1)
+    gram_start(2, field_rows, pf[pl.ds((1 - par) * 4, 4)].reshape(512, 256))
+    gram_x(2)
+    t_arrive(0)
+    t_begin(0)
+    t_begin(1)
+    t_arrive(2)
+    t_begin(4)
+    t_begin(5)
     gram_z(0)
-    for t in (0, 2, 1):
-        t_arrive(t)
-        t_begin(2 * t)
-        t_begin(2 * t + 1)
     gram_z(1)
+    t_arrive(1)
+    t_begin(2)
+    t_begin(3)
+    gram_z(2)
     for k in range(2):
         passed = fty.at[(y + (3, 1)[k]) % Y]
         arrived(passed, SEM["fy"] + k)
         part = fty.at[(y + (3, 1)[k]) % Y, pl.ds(128 * k, 128)]
         send(part, part, SEM["fy"] + 2 + k, at_y((1, 3)[k]))
+    t_cross(0, 0)
+    t_cross(0, 1)
+    t_cross(1, 0)
+    t_cross(1, 1)
     spin_total = gram_end(0)
-    for u in (0, 1, 4, 5):
-        t_cross(u, 0)
-        t_cross(u, 1)
-    field_total = gram_end(1)
+    ftot[:, pl.ds(pl.multiple_of(par * 512, 512), 512)] = gram_end(1)
+    ftot[:, pl.ds(pl.multiple_of((1 - par) * 512, 512), 512)] = gram_end(2)
+    field_total = ftot[...]
     gram_column = (spin_total / SPIN_SITES * (field_total / HIDDEN_UNITS)).astype(BF)
     factor = lax.dot_general(gram_column, dg[...], CONTRACT, preferred_element_type=F32)
     factor_out[...] = factor.astype(BF)
@@ -422,9 +450,14 @@
     u1[q] = jnp.sum(jnp.where(here, update, 0.0), axis=0, keepdims=True)
     for d in range(1, Q):
         send(u1.at[q], u1.at[q], SEM["uq"] + d, (wide, (q + d) % Q))
-    for u in (2, 3):
-        t_cross(u, 0)
-        t_cross(u, 1)
+    t_cross(4, 0)
+    t_cross(4, 1)
+    t_cross(5, 0)
+    t_cross(5, 1)
+    t_cross(2, 0)
+    t_cross(2, 1)
+    t_cross(3, 0)
+    t_cross(3, 1)
     for d in range(1, Q):
         arrived(u1.at[(q + Q - d) % Q], SEM["uq"] + d)
     u2[y, j] = jnp.sum(u1[...].reshape(Q, 128), axis=0, keepdims=True)
@@ -446,28 +479,44 @@
 
     mine_y = pl.ds(pl.multiple_of(y * 128, 128), 128)
 
-    def sites(i, k):
-        z1 = (z + FAR[i]) % Z
+    def sites(o, k):
         if k == 0:
-            return sp[z1, :, :, mine_y].reshape(512, 128)
-        return s2[z1, (y + k) % Y].reshape(512, 128)
-
-    for i in range(0, Z, 2):
+            return sp[toward(o), :, :, mine_y].reshape(512, 128)
+        return s2[toward(o), (y + k) % Y].reshape(512, 128)
+
+    def products(first, second):
         product = None
         for k in range(Y):
-            both = jnp.concatenate([sites(i, k), sites(i + 1, k)], axis=1)
+            both = jnp.concatenate([sites(first, k), sites(second, k)], axis=1)
             term = jnp.dot(wt[(y + k) % Y], both, preferred_element_type=F32)
             product = term if product is None else product + term
-        for n in range(2):
-            value = product[:, n * 128 : (n + 1) * 128].astype(BF)
-            off = FAR[i + n]
-            if off == 0:
-                r3[z] = value
-            else:
-                zb[i + n] = value
-                send(zb.at[i + n], r3.at[z], SEM["r3"] + off, at_z((z + off) % Z))
-    for d in range(1, Z):
-        arrived(r3.at[(z + d) % Z], SEM["r3"] + Z - d)
+        return product[:, :128], product[:, 128:]
+
+    def to_owner(o, value):
+        seen = {1: 1, 2: -2, -1: -1, -3: -3, -2: 2}[o]
+        zb[o + 3] = value.astype(BF)
+        send(zb.at[o + 3], r3.at[z], SEM["r3"] + 3 + seen, at_z(toward(o)))
+
+    for n in range(2):
+        away, near = products(4 - n, n - 3)
+        zb[7 - n] = away.astype(BF)
+        send(zb.at[7 - n], rel.at[n], SEM["rel"] + n, at_z(partner))
+        nearsum[n] = near
+
+    def relay_sum(n):
+        arrived(rel.at[n], SEM["rel"] + n)
+        to_owner(n - 3, nearsum[n] + rel[n].astype(F32))
+
+    ahead, behind = products(2, -1)
+    to_owner(2, ahead)
+    relay_sum(0)
+    to_owner(-1, behind)
+    ahead, own_term = products(1, 0)
+    r3[z] = own_term.astype(BF)
+    relay_sum(1)
+    to_owner(1, ahead)
+    for o in (-3, 2, -2, -1, 1):
+        arrived(r3.at[toward(o)], SEM["r3"] + 3 + o)
     for copy in sends:
         copy.wait_send()
 
@@ -502,6 +551,7 @@
             pltpu.VMEM((Y, Z, 1, 128), F32),
             pltpu.VMEM((8, 128, 128), BF),
             pltpu.VMEM((8, 128, 256), BF),
+            pltpu.VMEM((16, PANEL_ROWS), F32),
             pltpu.VMEM((2, 256, PANEL_ROWS), BF),
             pltpu.VMEM((2, 256, PANEL_ROWS), F32),
             pltpu.VMEM((2, 256, PANEL_ROWS), BF),
@@ -516,6 +566,8 @@
             pltpu.VMEM((Q, Y, 4, 128, 128), BF),
             pltpu.VMEM((Y, 256, 512), BF),
             pltpu.VMEM((Z, 256, 128), BF),
+            pltpu.VMEM((2, 256, 128), BF),
+            pltpu.VMEM((2, 256, 128), F32),
             pltpu.SemaphoreType.DMA((NSEM,)),
             pltpu.SemaphoreType.DMA((NSEM,)),
             pltpu.SemaphoreType.DMA((10,)),

time: 101 us -> 96 us (0.950)
  Pallas kernels: 98.9 us -> 93.6 us
    pallas_call x1, Pallas kernels: 96.9 us -> 91.5 us  [local(): pl.pallas_call(kernel, out_shape=(jax.ShapeDtypeStruct((Z, 256, 128), BF)...]
where the time goes in v4:
time: 96 us; the launch traced here: 94.9 us
  Pallas kernels  93.6 us (98%)
  between operations  1.29 us (1%)
    pallas_call x1, Pallas kernels, local(): pl.pallas_call(kernel, out_shape=(jax.ShapeDtypeStruct((Z, 256, 128), BF)...  91.5 us
    pallas_call x1, Pallas kernels, local(): pl.pallas_call(finish, out_shape=(jax.ShapeDtypeStruct((128, 1024), F32),...  2.07 us

profile of v4, /device:TPU:2, one launch (start us, length us, event | category | flops | bytes accessed | tf_op | source)
XLA Modules:
  0.0 94.9 jit_solution(11739885571397779696)
XLA Ops:
  1.3 91.5 %shard_map.85 = (bf16[8,256,128]{2,1,0:T(8,128)(2,1)}, bf16[16,1024]{1,0:T(8,128)(2,1)}, f32[1,128]{1,0:T(1,128)}) custom-call(s32[128,4096]{1,0:T(8,128)} %spins.1, bf16[128,1024]{1,0:T(8,128)(2,1)} %weights.1, f32[1,1024]{1,0:T(1,128)} %bitcast.1, bf16[128]{0:T(256)(128)(2,1)} %energy.1, s32[1]{0:T(128)S(6)} %copy.9.panel, bf16[1024,1024]{1,0:T(8,128)(2,1)} %diag.1), custom_call_target="tpu_custom_call" | custom-call | tf_op jit(solution)/shard_map/pallas_call | solution.py:536
  92.8 2.1 %shard_map.86 = (f32[128,1024]{1,0:T(8,128)}, bf16[16,1024]{1,0:T(8,128)(2,1)}, f32[16]{0:T(128)}) custom-call(bf16[8,256,128]{2,1,0:T(8,128)(2,1)} %get-tuple-element.6.terms, bf16[16,1024]{1,0:T(8,128)(2,1)} %get-tuple-element.7.factor, f32[1,128]{1,0:T(1,128)} %get-tuple-element.8.update), custom_call_target="tpu_custom_call" | custom-call | tf_op jit(solution)/shard_map/pallas_call | solution.py:586

commit v5 on v4

--- a/solution.py
+++ b/solution.py
@@ -509,10 +509,10 @@
 
     ahead, behind = products(2, -1)
     to_owner(2, ahead)
-    relay_sum(0)
     to_owner(-1, behind)
     ahead, own_term = products(1, 0)
     r3[z] = own_term.astype(BF)
+    relay_sum(0)
     relay_sum(1)
     to_owner(1, ahead)
     for o in (-3, 2, -2, -1, 1):

time: 96 us -> 95.8 us (level)
  no operation moved by 1% of the time
where the time goes in v5:
time: 95.8 us; the launch traced here: 94.9 us
  Pallas kernels  93.6 us (98%)
  between operations  1.29 us (1%)
    pallas_call x1, Pallas kernels, local(): pl.pallas_call(kernel, out_shape=(jax.ShapeDtypeStruct((Z, 256, 128), BF)...  91.5 us
    pallas_call x1, Pallas kernels, local(): pl.pallas_call(finish, out_shape=(jax.ShapeDtypeStruct((128, 1024), F32),...  2.07 us

profile of v5, /device:TPU:2, one launch (start us, length us, event | category | flops | bytes accessed | tf_op | source)
XLA Modules:
  0.0 94.9 jit_solution(3403327404723408142)
XLA Ops:
  1.3 91.5 %shard_map.85 = (bf16[8,256,128]{2,1,0:T(8,128)(2,1)}, bf16[16,1024]{1,0:T(8,128)(2,1)}, f32[1,128]{1,0:T(1,128)}) custom-call(s32[128,4096]{1,0:T(8,128)} %spins.1, bf16[128,1024]{1,0:T(8,128)(2,1)} %weights.1, f32[1,1024]{1,0:T(1,128)} %bitcast.1, bf16[128]{0:T(256)(128)(2,1)} %energy.1, s32[1]{0:T(128)S(6)} %copy.9.panel, bf16[1024,1024]{1,0:T(8,128)(2,1)} %diag.1), custom_call_target="tpu_custom_call" | custom-call | tf_op jit(solution)/shard_map/pallas_call | solution.py:536
  92.8 2.1 %shard_map.86 = (f32[128,1024]{1,0:T(8,128)}, bf16[16,1024]{1,0:T(8,128)(2,1)}, f32[16]{0:T(128)}) custom-call(bf16[8,256,128]{2,1,0:T(8,128)(2,1)} %get-tuple-element.6.terms, bf16[16,1024]{1,0:T(8,128)(2,1)} %get-tuple-element.7.factor, f32[1,128]{1,0:T(1,128)} %get-tuple-element.8.update), custom_call_target="tpu_custom_call" | custom-call | tf_op jit(solution)/shard_map/pallas_call | solution.py:586

commit v6 on v5

--- a/solution.py
+++ b/solution.py
@@ -524,9 +524,8 @@
 def finish(terms, factor, update, grad_out, factor_out, update_out):
     factor_out[...] = factor[...]
     update_out[...] = update[0, :16]
-    for jj in range(4):
-        block = terms[2 * jj].astype(F32) + terms[2 * jj + 1].astype(F32)
-        grad_out[:, jj * 256 : (jj + 1) * 256] = block.T / math.sqrt(SAMPLES)
+    block = terms[0].astype(F32) + terms[1].astype(F32)
+    grad_out[...] = block.T / math.sqrt(SAMPLES)
 
 
 def local(spins, weights, field_bias, energies, panel_index, diag_inverse):
@@ -590,8 +589,9 @@
             jax.ShapeDtypeStruct((16, PANEL_ROWS), BF),
             jax.ShapeDtypeStruct((16,), F32),
         ),
-        in_specs=[vmem, vmem, vmem],
-        out_specs=(vmem, vmem, vmem),
+        grid=(4,),
+        in_specs=[pl.BlockSpec((2, 256, 128), lambda i: (i, 0, 0)), vmem, vmem],
+        out_specs=(pl.BlockSpec((128, 256), lambda i: (0, i)), vmem, vmem),
     )(terms, factor, update)
 
 

time: 95.8 us -> 97.1 us (1.014)
  Pallas kernels: 93.6 us -> 94.9 us
    pallas_call x1, Pallas kernels: 2.07 us -> 3.37 us  [local(): pl.pallas_call(finish, out_shape=(jax.ShapeDtypeStruct((128, 1024), F32),...]
where the time goes in v6:
time: 97.1 us; the launch traced here: 96.2 us
  Pallas kernels  94.9 us (98%)
  between operations  1.29 us (1%)
    pallas_call x1, Pallas kernels, local(): pl.pallas_call(kernel, out_shape=(jax.ShapeDtypeStruct((Z, 256, 128), BF)...  91.5 us
    pallas_call x1, Pallas kernels, local(): pl.pallas_call(finish, out_shape=(jax.ShapeDtypeStruct((128, 1024), F32),...  3.37 us

profile of v6, /device:TPU:2, one launch (start us, length us, event | category | flops | bytes accessed | tf_op | source)
XLA Modules:
  0.0 96.2 jit_solution(11398790202143942839)
XLA Ops:
  1.3 91.5 %shard_map.85 = (bf16[8,256,128]{2,1,0:T(8,128)(2,1)}, bf16[16,1024]{1,0:T(8,128)(2,1)}, f32[1,128]{1,0:T(1,128)}) custom-call(s32[128,4096]{1,0:T(8,128)} %spins.1, bf16[128,1024]{1,0:T(8,128)(2,1)} %weights.1, f32[1,1024]{1,0:T(1,128)} %bitcast.1, bf16[128]{0:T(256)(128)(2,1)} %energy.1, s32[1]{0:T(128)S(6)} %copy.9.panel, bf16[1024,1024]{1,0:T(8,128)(2,1)} %diag.1), custom_call_target="tpu_custom_call" | custom-call | tf_op jit(solution)/shard_map/pallas_call | solution.py:535
  92.8 3.4 %shard_map.86 = (f32[128,1024]{1,0:T(8,128)}, bf16[16,1024]{1,0:T(8,128)(2,1)}, f32[16]{0:T(128)}) custom-call(bf16[8,256,128]{2,1,0:T(8,128)(2,1)} %get-tuple-element.6.terms, bf16[16,1024]{1,0:T(8,128)(2,1)} %get-tuple-element.7.factor, f32[1,128]{1,0:T(1,128)} %get-tuple-element.8.update), custom_call_target="tpu_custom_call" | custom-call | tf_op jit(solution)/shard_map/pallas_call | solution.py:585
